TPU v7x, 32 devices: a whole 2x2x4 slice. The times are simulated.
32 devices in a mesh: rep: 2 (over y), row: 4 (over z), col: 4 (over x, core).
Axes of the slice: x: 2, y: 2, z: 4, core: 2. Of those that a mesh axis runs over, the one named last changes fastest.
Arguments:
- grads: bfloat16 [2, 4096, 4096], P('rep', 'row', 'col'), may hold values from -4 to 4
- left_basis: float32 [4, 1024, 4096], P(None, 'rep', 'row'), may hold values from -0.09375 to 0.09375
- right_basis: float32 [4, 1024, 4096], P(None, 'rep', 'col'), may hold values from -0.09375 to 0.09375
- eigen_left: float32 [4096], P('row'), may hold values from 0.05 to 5
- eigen_right: float32 [4096], P('col'), may hold values from 0.05 to 5
Outputs:
- update: bfloat16 [4096, 4096], P('row', 'col')
All inputs are finite; a program needn't handle non-finite values.
Results may differ from a plain program's by a relative error of at most 0.001.
Values may be sent and summed in bfloat16 or wider, within the bound.
A program may use at most 128 MiB of HBM per device.

v0:
```python
import jax
import jax.numpy as jnp
from jax import lax
from jax.sharding import PartitionSpec as P

epsilon = 1e-06


def body(grads, left_basis, right_basis, eigen_left, eigen_right):
    highest = lax.Precision.HIGHEST
    contract_first = (((0,), (0,)), ((), ()))
    contract_last = (((1,), (1,)), ((), ()))
    arrived = lax.all_to_all(grads, "rep", split_axis=1, concat_axis=0, tiled=True)
    summed = jnp.sum(arrived.astype(jnp.float32), axis=0)
    stacked = lax.all_gather(summed, "row", axis=0, tiled=True)
    left_piece = left_basis.reshape(-1, left_basis.shape[2])
    right_piece = right_basis.reshape(-1, right_basis.shape[2])
    left_done = lax.psum_scatter(
        lax.dot_general(stacked, left_piece, contract_first, precision=highest),
        "rep",
        scatter_dimension=0,
        tiled=True,
    )
    gathered = lax.all_gather(left_done, "col", axis=0, tiled=True)
    row_share = gathered.shape[1] // lax.axis_size("rep")
    block = gathered
    rotated = lax.psum_scatter(
        lax.dot_general(block, right_piece, contract_first, precision=highest),
        "rep",
        scatter_dimension=0,
        tiled=True,
    )
    offset = lax.axis_index("rep") * row_share
    left_eigen = lax.dynamic_slice_in_dim(eigen_left, offset, row_share)
    scaled_share = rotated / (left_eigen[:, None] + eigen_right[None, :] + epsilon)
    scaled = lax.all_gather(scaled_share, "rep", axis=0, tiled=True)
    block = right_piece
    back_share = lax.psum_scatter(
        lax.dot_general(block, scaled, contract_last, precision=highest),
        "col",
        scatter_dimension=0,
        tiled=True,
    )
    back_full = lax.all_gather(back_share, "rep", axis=0, tiled=True)
    block = left_piece
    out_share = lax.psum_scatter(
        lax.dot_general(block, back_full, contract_last, precision=highest),
        "row",
        scatter_dimension=0,
        tiled=True,
    ).astype(jnp.bfloat16)
    return lax.all_gather(out_share, "rep", axis=0, tiled=True)


def solution(mesh):
    placed = (
        P("rep", "row", "col"),
        P(None, "rep", "row"),
        P(None, "rep", "col"),
        P("row"),
        P("col"),
    )
    return jax.shard_map(
        body, mesh=mesh, in_specs=placed, out_specs=P("row", "col"), check_vma=False
    )
```

profile of v0, /device:TPU:0, one launch (start us, length us, event | category | flops | bytes accessed | tf_op | source)
XLA Modules:
  0.0 918.3 jit_solution(16239645875025765021)
XLA Ops:
  6.5 6.8 copy.13
  13.8 12.8 %reduce = bf16[1024,1024]{1,0:T(8,128)(2,1)S(1)} reduce(bf16[1024,1,1024]{2,1,0:T(2,128)(2,1)} %bitcast.20, bf16[]{:T(256)} %broadcast.2), dimensions={1}, to_apply=%bitcast.19.reduce_sub_computation | reduce | bytes 4194306
  26.6 2.5 reshape.16
  29.1 30.1 %all_to_all.4 = bf16[2,2,262144]{2,1,0:T(2,128)(2,1)S(1)} all-to-all(bf16[2,2,262144]{2,1,0:T(2,128)(2,1)} %reshape.16), channel_id=1, replica_groups=mesh['rep'=2,'row'=4,'col'=4] {'rep'}, dimensions={0} | all-to-all | bytes 4194304 | tf_op jit(solution)/shard_map/all_to_all | solution.py:13
  59.2 3.1 reshape.17
  62.3 3.0 copy.10
  65.3 1.8 convert_reduce_fusion
  67.4 150.0 %all-gather.6.cloned.1.call-done = f32[2048,1024]{1,0:T(8,128)} async-done(((f32[512,1024]{1,0:T(8,128)}), f32[2048,1024]{1,0:T(8,128)}) %all-gather.6.cloned.1.call-update) | async-done | bytes 8388624 | tf_op jit(solution)/shard_map/all_gather | solution.py:15
  217.4 31.6 %fusion = f32[1024,1024]{1,0:T(8,128)} fusion(f32[2048,1024]{1,0:T(8,128)} %all-gather.6.cloned.1.call-done, f32[2048,1024]{1,0:T(8,128)} %bitcast.25), kind=kOutput, calls=%fused_computation.5 | convolution fusion | flops 25769803776 | bytes 20971520 | tf_op jit(solution)/shard_map/dot_general | solution.py:19
  249.1 52.6 %reduce-scatter.5.cloned.1.call-done = f32[512,1024]{1,0:T(8,128)} async-done(((f32[1024,1024]{1,0:T(8,128)}), f32[512,1024]{1,0:T(8,128)}) %reduce-scatter.5.cloned.1.call-update) | async-done | bytes 2097168 | tf_op jit(solution)/shard_map/reduce_scatter | solution.py:18
  302.0 59.6 %all-gather.8.cloned.1.call-done = f32[2048,1024]{1,0:T(8,128)} async-done(((f32[512,1024]{1,0:T(8,128)}), f32[2048,1024]{1,0:T(8,128)}) %all-gather.8.cloned.1.call-update) | async-done | bytes 8388624 | tf_op jit(solution)/shard_map/all_gather | solution.py:24
  361.7 31.6 %fusion.1 = f32[1024,1024]{1,0:T(8,128)} fusion(f32[2048,1024]{1,0:T(8,128)} %all-gather.8.cloned.1.call-done, f32[2048,1024]{1,0:T(8,128)} %bitcast.23), kind=kOutput, calls=%fused_computation.6 | convolution fusion | flops 25769803776 | bytes 20971520 | tf_op jit(solution)/shard_map/dot_general | solution.py:28
  393.4 0.6 copy-done.1
  394.1 53.7 %reduce-scatter.7.cloned.1.call-done = f32[512,1024]{1,0:T(8,128)} async-done(((f32[1024,1024]{1,0:T(8,128)}), f32[512,1024]{1,0:T(8,128)}) %reduce-scatter.7.cloned.1.call-update) | async-done | bytes 2097168 | tf_op jit(solution)/shard_map/reduce_scatter | solution.py:27
  447.8 3.3 add_divide_fusion
  451.6 56.4 %all-gather.10.cloned.1.call-done = f32[1024,1024]{1,0:T(8,128)} async-done(((f32[512,1024]{1,0:T(8,128)}), f32[1024,1024]{1,0:T(8,128)}) %all-gather.10.cloned.1.call-update) | async-done | bytes 4194320 | tf_op jit(solution)/shard_map/all_gather | solution.py:36
  508.0 31.0 %convolution_bitcast_fusion.1 = f32[2048,1024]{0,1:T(8,128)} fusion(f32[1024,1024]{1,0:T(8,128)} %all-gather.10.cloned.1.call-done, f32[2048,1024]{1,0:T(8,128)} %bitcast.24), kind=kOutput, calls=%fused_computation.1 | convolution fusion | flops 25769803776 | bytes 20971520 | tf_op jit(solution)/shard_map/dot_general | solution.py:39
  539.1 71.8 %reduce-scatter.9.cloned.1.call-done = f32[512,1024]{0,1:T(8,128)} async-done(((f32[2048,1024]{0,1:T(8,128)}), f32[512,1024]{0,1:T(8,128)}) %reduce-scatter.9.cloned.1.call-update) | async-done | bytes 2097168 | tf_op jit(solution)/shard_map/reduce_scatter | solution.py:38
  611.0 58.3 %all-gather.12.cloned.1.call-done = f32[1024,1024]{0,1:T(8,128)} async-done(((f32[512,1024]{0,1:T(8,128)}), f32[1024,1024]{0,1:T(8,128)}) %all-gather.12.cloned.1.call-update) | async-done | bytes 4194320 | tf_op jit(solution)/shard_map/all_gather | solution.py:44
  669.3 57.0 %convolution_bitcast_fusion = f32[2048,1024]{0,1:T(8,128)} fusion(f32[1024,1024]{0,1:T(8,128)} %all-gather.12.cloned.1.call-done, f32[2048,1024]{1,0:T(8,128)} %bitcast.26), kind=kOutput, calls=%fused_computation | convolution fusion | flops 25769803776 | bytes 20971520 | tf_op jit(solution)/shard_map/dot_general | solution.py:47
  726.4 144.6 %reduce-scatter.11.cloned.1.call-done = f32[512,1024]{0,1:T(8,128)} async-done(((f32[2048,1024]{0,1:T(8,128)}), f32[512,1024]{0,1:T(8,128)}) %reduce-scatter.11.cloned.1.call-update) | async-done | bytes 2097168 | tf_op jit(solution)/shard_map/reduce_scatter | solution.py:46
  870.9 2.7 convert_element_type.14
  873.7 34.0 %all-gather.14.cloned.1.call-done = bf16[1024,1024]{0,1:T(8,128)(2,1)} async-done(((bf16[512,1024]{0,1:T(8,128)(2,1)}), bf16[1024,1024]{0,1:T(8,128)(2,1)}) %all-gather.14.cloned.1.call-update) | async-done | bytes 2097168 | tf_op jit(solution)/shard_map/all_gather | solution.py:52
  907.6 3.9 copy.11
  (23 shorter events, 2.0 us)
Async XLA Ops:
  6.5 210.9 %all-gather.6.cloned.1.call-start = ((), (), s32[]{:S(2)}) async-start(), calls=%async_computation.5 | async-start | bytes 10485760 | tf_op jit(solution)/shard_map/all_gather | solution.py:15
  67.1 234.6 %reduce-scatter.5.cloned.1.call-start = ((), (), s32[]{:S(2)}) async-start(), calls=%async_computation.6 | async-start | bytes 6291456 | tf_op jit(solution)/shard_map/reduce_scatter | solution.py:18
  249.0 112.6 %all-gather.8.cloned.1.call-start = ((), (), s32[]{:S(2)}) async-start(), calls=%async_computation.7 | async-start | bytes 10485760 | tf_op jit(solution)/shard_map/all_gather | solution.py:24
  301.8 146.1 %reduce-scatter.7.cloned.1.call-start = ((), (), s32[]{:S(2)}) async-start(), calls=%async_computation.8 | async-start | bytes 6291456 | tf_op jit(solution)/shard_map/reduce_scatter | solution.py:27
  393.3 0.7 copy-start.1
  393.3 54.5 %copy-start = (f32[1024]{0:T(1024)S(1)}, f32[1024]{0:T(1024)}, u32[]{:S(2)}) copy-start(f32[1024]{0:T(1024)} %param.9) | copy-start | bytes 12292
  393.3 114.7 %all-gather.10.cloned.1.call-start = ((), (), s32[]{:S(2)}) async-start(), calls=%async_computation.9 | async-start | bytes 6291456 | tf_op jit(solution)/shard_map/all_gather | solution.py:36
  451.1 159.8 %reduce-scatter.9.cloned.1.call-start = ((), (), s32[]{:S(2)}) async-start(), calls=%async_computation.10 | async-start | bytes 10485760 | tf_op jit(solution)/shard_map/reduce_scatter | solution.py:38
  539.1 130.3 %all-gather.12.cloned.1.call-start = ((), (), s32[]{:S(2)}) async-start(), calls=%async_computation.11 | async-start | bytes 6291456 | tf_op jit(solution)/shard_map/all_gather | solution.py:44
  611.0 260.0 %reduce-scatter.11.cloned.1.call-start = ((), (), s32[]{:S(2)}) async-start(), calls=%async_computation.12 | async-start | bytes 10485760 | tf_op jit(solution)/shard_map/reduce_scatter | solution.py:46
  726.3 181.3 %all-gather.14.cloned.1.call-start = ((), (), s32[]{:S(2)}) async-start(), calls=%async_computation.13 | async-start | bytes 3145728 | tf_op jit(solution)/shard_map/all_gather | solution.py:52
Sparse Core Ops, SparseCore 0:
  67.2 150.1 all-gather.5
  249.2 52.5 reduce-scatter.4
  303.4 58.2 all-gather.7
  393.5 54.3 reduce-scatter.6
  451.2 56.7 all-gather.9
  539.2 71.7 reduce-scatter.8
  612.5 56.7 all-gather.11
  726.4 144.4 reduce-scatter.10
  873.8 33.8 all-gather.13
where the time goes:
time: 925 us; the launch traced here: 918 us
  waiting for transfers between devices  681 us (74%)
  matrix products  151 us (16%)
  blocking collectives  30.1 us (3%)
  local copies, waits for them, and re-layouts  20.5 us (2%)
  other arithmetic  20.5 us (2%)
  between operations  13.4 us (1%)
    all_gather x1, waiting for transfers between devices, body(): stacked = lax.all_gather(summed, 'row', axis=0, tiled=True)  150 us
    reduce_scatter x1, waiting for transfers between devices, body(): lax.psum_scatter(lax.dot_general(block, back_full, contract_last, precisi...  145 us
    reduce_scatter x1, waiting for transfers between devices, body(): lax.psum_scatter(lax.dot_general(block, scaled, contract_last, precision=...  71.8 us
    all_gather x1, waiting for transfers between devices, body(): gathered = lax.all_gather(left_done, 'col', axis=0, tiled=True)  59.6 us
    all_gather x1, waiting for transfers between devices, body(): back_full = lax.all_gather(back_share, 'rep', axis=0, tiled=True)  58.3 us
    dot_general x1, matrix products, body(): lax.dot_general(block, back_full, contract_last, precision=highest)  57 us
    all_gather x1, waiting for transfers between devices, body(): scaled = lax.all_gather(scaled_share, 'rep', axis=0, tiled=True)  56.4 us
    reduce_scatter x1, waiting for transfers between devices, body(): lax.psum_scatter(lax.dot_general(block, right_piece, contract_first, prec...  53.7 us
  transfers between devices with their start and end apart: 9, of which 9 were waited for; matrix products, arithmetic and copies ran while one was open for 0% of the time, Pallas kernels for 0%

commit v1 on v0

--- a/solution.py
+++ b/solution.py
@@ -52,6 +52,146 @@
     return lax.all_gather(out_share, "rep", axis=0, tiled=True)
 
 
+CHUNKS_IN = 2
+CHUNKS_MID = 2
+CHUNKS_OUT = 2
+GROUP = 128
+SPAN = 240.0
+LOW = -120.0
+contract_first = (((0,), (0,)), ((), ()))
+contract_last = (((1,), (1,)), ((), ()))
+
+
+def matmul(a, b, dims):
+    return lax.dot_general(
+        a, b, dims, precision=lax.Precision.HIGH, preferred_element_type=jnp.float32
+    )
+
+
+def encode(x):
+    rows, columns = x.shape
+    groups = rows // GROUP
+    top = jnp.max(jnp.abs(x).reshape(groups, GROUP, columns), axis=1)
+    top = lax.reduce_precision(jnp.maximum(top, 1e-30) * 1.0078125, 8, 7)
+    per_row = jnp.broadcast_to(
+        (SPAN / top)[:, None, :], (groups, GROUP, columns)
+    ).reshape(rows, columns)
+    power = jnp.exp2(jnp.abs(x) * per_row + LOW)
+    code = jnp.where(x < 0, -power, power).astype(jnp.bfloat16)
+    scale = jnp.pad(top.astype(jnp.bfloat16), ((0, 16 - groups), (0, 0)))
+    return jnp.concatenate([code, scale], axis=0)
+
+
+def decode(coded):
+    rows, columns = coded.shape[0] - 16, coded.shape[1]
+    groups = rows // GROUP
+    code = coded[:rows].astype(jnp.float32)
+    top = coded[rows : rows + groups].astype(jnp.float32) * (1.0 / SPAN)
+    per_row = jnp.broadcast_to(top[:, None, :], (groups, GROUP, columns)).reshape(
+        rows, columns
+    )
+    size = (jnp.log2(jnp.abs(code)) - LOW) * per_row
+    return jnp.where(code < 0, -size, size)
+
+
+def shift(x, axis, step):
+    n = lax.axis_size(axis)
+    return lax.ppermute(x, axis, [(s, (s + step) % n) for s in range(n)])
+
+
+def half(x, index, axis):
+    size = x.shape[axis] // 2
+    return lax.dynamic_slice_in_dim(x, index * size, size, axis)
+
+
+def ordered(mine, peer, me, axis):
+    return jnp.concatenate(
+        [jnp.where(me == 0, mine, peer), jnp.where(me == 0, peer, mine)], axis=axis
+    )
+
+
+def scatter_blocks(blocks, axis, finish):
+    n = lax.axis_size(axis)
+    i = lax.axis_index(axis)
+    sent = []
+    for step in range(1, n):
+        block = lax.dynamic_index_in_dim(blocks, lax.rem(i + step, n), 0, False)
+        sent.append(shift(encode(block), axis, step))
+    total = lax.dynamic_index_in_dim(blocks, i, 0, False)
+    for got in sent:
+        total = total + decode(got)
+    return finish(total)
+
+
+def pair_body(grads, left_basis, right_basis, eigen_left, eigen_right):
+    me = lax.axis_index("rep")
+    col = lax.axis_index("col")
+    cols = lax.axis_size("col")
+    blocks, tall, wide = left_basis.shape
+    columns = right_basis.shape[2]
+
+    grad = grads[0]
+    keep, give = half(grad, me, 1), half(grad, 1 - me, 1)
+    width = keep.shape[1] // CHUNKS_IN
+    coded = []
+    for c in range(CHUNKS_IN):
+        at = slice(c * width, (c + 1) * width)
+        got = shift(give[:, at], "rep", 1)
+        coded.append(encode(keep[:, at].astype(jnp.float32) + got.astype(jnp.float32)))
+
+    share = lax.dynamic_index_in_dim(left_basis, col, 0, False)
+    share = shift(encode(share), "rep", 1)
+    shares = [share] + [shift(share, "col", s) for s in range(1, cols)]
+    rolled = jnp.stack([decode(s) for s in shares])
+    place = lax.rem(col - jnp.arange(blocks) + cols, cols)
+    other = jnp.take(rolled, place, axis=0, mode="clip")
+    left = ordered(left_basis, other, me, 1).reshape(-1, wide)
+
+    right = right_basis
+    lines = right.shape[1]
+    rotated = 0.0
+    for c in range(CHUNKS_IN):
+        stacked = lax.all_gather(coded[c], "row", axis=0)
+        stacked = jnp.concatenate([decode(s) for s in stacked], axis=0)
+        part = encode(matmul(stacked, left, contract_first))
+        gathered = lax.all_gather(part, "col", axis=0)
+        gathered = jnp.concatenate([decode(s) for s in gathered], axis=0)
+        w = lines // CHUNKS_IN
+        r = right[:, c * w : (c + 1) * w].reshape(-1, columns)
+        rotated = rotated + matmul(gathered, r, contract_first)
+
+    eigen = eigen_left[:, None] + eigen_right[None, :] + epsilon
+    eigen = half(eigen, me, 0)
+    keep, give = half(rotated, me, 0), half(rotated, 1 - me, 0)
+    right_flat = right.reshape(-1, columns)
+    high = keep.shape[0] // CHUNKS_MID
+    backs = []
+    for c in range(CHUNKS_MID):
+        at = slice(c * high, (c + 1) * high)
+        got = shift(encode(give[at]), "rep", 1)
+        mine = (keep[at] + decode(got)) / eigen[at]
+        peer = decode(shift(encode(mine), "rep", 1))
+        scaled = ordered(mine, peer, me, 0)
+        back = matmul(right_flat, scaled, contract_last)
+        back = back.reshape(cols, -1, back.shape[1])
+        backs.append(scatter_blocks(back, "col", lambda t: t))
+    back = jnp.concatenate(
+        [b[:, s * high : (s + 1) * high] for s in range(2) for b in backs], axis=1
+    )
+
+    narrow = back.shape[0] // CHUNKS_OUT
+    mine, peer = [], []
+    for c in range(CHUNKS_OUT):
+        out = matmul(left, back[c * narrow : (c + 1) * narrow], contract_last)
+        out = out.reshape(blocks, -1, narrow)
+        done = scatter_blocks(out, "row", lambda t: t.astype(jnp.bfloat16))
+        mine.append(done)
+        peer.append(shift(done, "rep", 1))
+    return ordered(
+        jnp.concatenate(mine, axis=1), jnp.concatenate(peer, axis=1), me, 1
+    )
+
+
 def solution(mesh):
     placed = (
         P("rep", "row", "col"),
@@ -61,5 +201,9 @@
         P("col"),
     )
     return jax.shard_map(
-        body, mesh=mesh, in_specs=placed, out_specs=P("row", "col"), check_vma=False
-    )
+        pair_body if mesh.shape["rep"] == 2 else body,
+        mesh=mesh,
+        in_specs=placed,
+        out_specs=P("row", "col"),
+        check_vma=False,
+    )

time: 925 us -> 562 us (0.61)
  waiting for transfers between devices: 681 us -> 237 us
  other arithmetic: 20.5 us -> 104 us
  matrix products: 151 us -> 78 us
  local copies, waits for them, and re-layouts: 20.5 us -> 76.5 us
  starting transfers between devices: 1.26 us -> 41.3 us
  blocking collectives: 30.1 us -> 0 us
    all_gather x5 -> x4, waiting for transfers between devices: 358 us -> 18.4 us  [the longest x2 18.4 us: pair_body(): gathered = lax.all_gather(part, 'col', axis=0)]
    reduce_scatter x4 -> x0, waiting for transfers between devices: 323 us -> none  [the longest x1 145 us: body(): lax.psum_scatter(lax.dot_general(block, back_full, contract_last, precisi...]
    ppermute x0 -> x24, waiting for transfers between devices: none -> 218 us  [shift(): return lax.ppermute(x, axis, [(s, (s + step) % n) for s in range(n)])]
    dot_general x4 -> x8, matrix products: 151 us -> 78 us  [matmul(): lax.dot_general(a, b, dims, precision=lax.Precision.HIGH, preferred_eleme...]
    all_to_all x1 -> x0, blocking collectives: 30.1 us -> none  [body(): lax.all_to_all(grads, 'rep', split_axis=1, concat_axis=0, tiled=True)]
    ppermute x0 -> x24, starting transfers between devices: none -> 28.7 us  [shift(): return lax.ppermute(x, axis, [(s, (s + step) % n) for s in range(n)])]
    dynamic_slice x1 -> x5, local copies, waits for them, and re-layouts: 0.07 us -> 27.2 us  [the longest x1 20.6 us: scatter_blocks(): block = lax.dynamic_index_in_dim(blocks, lax.rem(i + step, n), 0, False)]
    select_n x0 -> x8, other arithmetic: none -> 20.4 us  [the longest x4 10.2 us: ordered(): jnp.where(me == 0, mine, peer)]
  transfers between devices with their start and end apart: 9 -> 28, of which waited for: 9 -> 15; matrix products, arithmetic and copies ran while one was open for 0% -> 27% of each run, Pallas kernels for 0% -> 0%
where the time goes in v1:
time: 562 us; the launch traced here: 551 us
  waiting for transfers between devices  237 us (42%)
  other arithmetic  104 us (19%)
  matrix products  78 us (14%)
  local copies, waits for them, and re-layouts  76.5 us (14%)
  starting transfers between devices  41.3 us (7%)
  between operations  14.1 us (3%)
    ppermute x24, waiting for transfers between devices, shift(): return lax.ppermute(x, axis, [(s, (s + step) % n) for s in range(n)])  218 us
    dot_general x8, matrix products, matmul(): lax.dot_general(a, b, dims, precision=lax.Precision.HIGH, preferred_eleme...  78 us
    ppermute x24, starting transfers between devices, shift(): return lax.ppermute(x, axis, [(s, (s + step) % n) for s in range(n)])  28.7 us
    unnamed x35, local copies, waits for them, and re-layouts  20.7 us
    dynamic_slice x1, local copies, waits for them, and re-layouts, scatter_blocks(): block = lax.dynamic_index_in_dim(blocks, lax.rem(i + step, n), 0, False)  20.6 us
    all_gather x2, waiting for transfers between devices, pair_body(): gathered = lax.all_gather(part, 'col', axis=0)  18.4 us
    convert_element_type x15, other arithmetic, encode(): code = jnp.where(x < 0, -power, power).astype(jnp.bfloat16)  14.5 us
    all_gather x2, starting transfers between devices, pair_body(): gathered = lax.all_gather(part, 'col', axis=0)  12.5 us
  transfers between devices with their start and end apart: 28, of which 15 were waited for; matrix products, arithmetic and copies ran while one was open for 27% of the time, Pallas kernels for 0%

profile of v1, /device:TPU:0, one launch (start us, length us, event | category | flops | bytes accessed | tf_op | source)
XLA Modules:
  0.0 550.8 jit_solution(15245038209902669149)
XLA Ops:
  11.4 12.7 %collective-permute-done.4 = bf16[1024,256]{1,0:T(8,128)(2,1)S(1)} collective-permute-done((bf16[1024,256]{1,0:T(8,128)(2,1)S(1)}, bf16[1024,256]{1,0:T(8,128)(2,1)S(1)}, u32[]{:S(2)}, u32[]{:S(2)}) %collective-permute-start.4) | collective-permute-done | bytes 524320 | tf_op jit(solution)/shard_map/ppermute | solution.py:99
  24.1 10.4 %collective-permute-done.5 = bf16[1024,256]{1,0:T(8,128)(2,1)S(1)} collective-permute-done((bf16[1024,256]{1,0:T(8,128)(2,1)S(1)}, bf16[1024,256]{1,0:T(8,128)(2,1)S(1)}, u32[]{:S(2)}, u32[]{:S(2)}) %collective-permute-start.5) | collective-permute-done | bytes 524320 | tf_op jit(solution)/shard_map/ppermute | solution.py:99
  42.9 23.3 %collective-permute-done = bf16[528,1024]{1,0:T(8,128)(2,1)S(1)} collective-permute-done((bf16[528,1024]{1,0:T(8,128)(2,1)S(1)}, bf16[528,1024]{1,0:T(8,128)(2,1)S(1)}, u32[]{:S(2)}, u32[]{:S(2)}) %collective-permute-start) | collective-permute-done | bytes 1081376 | tf_op jit(solution)/shard_map/ppermute | solution.py:99
  71.0 20.8 %collective-permute-done.1 = bf16[528,1024]{1,0:T(8,128)(2,1)} collective-permute-done((bf16[528,1024]{1,0:T(8,128)(2,1)S(1)}, bf16[528,1024]{1,0:T(8,128)(2,1)}, u32[]{:S(2)}, u32[]{:S(2)}) %collective-permute-start.1) | collective-permute-done | bytes 1081376 | tf_op jit(solution)/shard_map/ppermute | solution.py:99
  97.2 17.2 %collective-permute-done.3 = bf16[528,1024]{1,0:T(8,128)(2,1)} collective-permute-done((bf16[528,1024]{1,0:T(8,128)(2,1)S(1)}, bf16[528,1024]{1,0:T(8,128)(2,1)}, u32[]{:S(2)}, u32[]{:S(2)}) %collective-permute-start.3) | collective-permute-done | bytes 1081376 | tf_op jit(solution)/shard_map/ppermute | solution.py:99
  120.7 7.7 %gather_fusion = f32[4,512,1024]{2,1,0:T(8,128)} fusion(f32[4,512,1024]{2,1,0:T(8,128)} %pad_maximum_fusion.1, s32[1024]{0:T(1024)S(1)} %pad_clamp_fusion), kind=kCustom, calls=%fused_computation | custom fusion | bytes 16777232 | tf_op jit(solution)/shard_map/jit(_take)/gather | solution.py:147
  150.7 11.2 %bitcast_reduce_fusion.4 = (f32[2,1024]{1,0:T(2,128)S(1)}, f32[256,1024]{1,0:T(8,128)S(1)}) fusion(f32[4096,1024]{1,0:T(8,128)} %bitcast.615, f32[1024,256]{1,0:T(8,128)S(1)} %get-tuple-element.58, f32[1024,256]{1,0:T(8,128)S(1)} %get-tuple-element.59, f32[1024,256]{1,0:T(8,128)S(1)} %get-tuple-element.60, f32[1024,256]{1,0:T(8,128)S(1)} %get-tuple-element.57), kind=kOutput, calls=%fused_computation.489 | convolution fusion | flops 6446118912 | bytes 22028288 | tf_op jit(solution)/shard_map/dot_general | solution.py:66
  163.3 12.1 %all-gather.11.cloned.1.call-start = ((), (), s32[]{:S(2)}) async-start(), calls=%async_computation.1 | async-start | bytes 2785280 | tf_op jit(solution)/shard_map/all_gather | solution.py:157
  179.0 11.3 %bitcast_reduce_fusion.6 = (f32[2,1024]{1,0:T(2,128)S(1)}, f32[256,1024]{1,0:T(8,128)S(1)}) fusion(f32[4096,1024]{1,0:T(8,128)} %bitcast.616, f32[1024,256]{1,0:T(8,128)S(1)} %get-tuple-element.66, f32[1024,256]{1,0:T(8,128)S(1)} %get-tuple-element.67, f32[1024,256]{1,0:T(8,128)S(1)} %get-tuple-element.68, f32[1024,256]{1,0:T(8,128)S(1)} %get-tuple-element.65), kind=kOutput, calls=%fused_computation.499 | convolution fusion | flops 6446118912 | bytes 22028288 | tf_op jit(solution)/shard_map/dot_general | solution.py:66
  191.5 8.4 %fusion.419 = (f32[4,256,1024]{2,1,0:T(8,128)}, f32[4,256,1024]{2,1,0:T(8,128)}) fusion(f32[4,512,1024]{2,1,0:T(8,128)} %param.7), kind=kLoop, calls=%fused_computation.681 | loop fusion | bytes 16777216 | tf_op jit(solution)/shard_map/slice | solution.py:160
  200.7 18.4 %all-gather.11.cloned.1.call-done = bf16[1088,1024]{1,0:T(8,128)(2,1)} async-done(((bf16[272,1024]{1,0:T(8,128)(2,1)}), bf16[1088,1024]{1,0:T(8,128)(2,1)}) %all-gather.11.cloned.1.call-update) | async-done | bytes 2228240 | tf_op jit(solution)/shard_map/all_gather | solution.py:157
  232.4 7.4 %fusion.63 = f32[1024,1024]{1,0:T(8,128)S(1)} fusion(f32[1024,1024]{1,0:T(8,128)S(1)} %fusion.8, f32[1024,1024]{1,0:T(8,128)S(1)} %bitcast.621, f32[256,1024]{1,0:T(8,128)S(1)} %get-tuple-element.42, f32[256,1024]{1,0:T(8,128)S(1)} %get-tuple-element.43, f32[256,1024]{1,0:T(8,128)S(1)} %get-tuple-element.44, f32[256,1024]{1,0:T(8,128)S(1)} %get-tuple-element.41), kind=kOutput, calls=%fused_computation.89 | convolution fusion | flops 6446645248 | bytes 16777216 | tf_op jit(solution)/shard_map/dot_general | solution.py:66
  244.3 13.0 %collective-permute-done.11 = bf16[272,1024]{1,0:T(8,128)(2,1)S(1)} collective-permute-done((bf16[272,1024]{1,0:T(8,128)(2,1)S(1)}, bf16[272,1024]{1,0:T(8,128)(2,1)S(1)}, u32[]{:S(2)}, u32[]{:S(2)}) %collective-permute-start.11) | collective-permute-done | bytes 557088 | tf_op jit(solution)/shard_map/ppermute | solution.py:99
  257.3 11.2 %collective-permute-done.6 = bf16[272,1024]{1,0:T(8,128)(2,1)S(1)} collective-permute-done((bf16[272,1024]{1,0:T(8,128)(2,1)S(1)}, bf16[272,1024]{1,0:T(8,128)(2,1)S(1)}, u32[]{:S(2)}, u32[]{:S(2)}) %collective-permute-start.6) | collective-permute-done | bytes 557088 | tf_op jit(solution)/shard_map/ppermute | solution.py:99
  274.1 13.2 %collective-permute-done.7 = bf16[272,1024]{1,0:T(8,128)(2,1)} collective-permute-done((bf16[272,1024]{1,0:T(8,128)(2,1)S(1)}, bf16[272,1024]{1,0:T(8,128)(2,1)}, u32[]{:S(2)}, u32[]{:S(2)}) %collective-permute-start.7) | collective-permute-done | bytes 557088 | tf_op jit(solution)/shard_map/ppermute | solution.py:99
  289.4 10.7 %convolution_bitcast_fusion.1 = f32[2048,512]{0,1:T(8,128)} fusion(f32[2048,1024]{1,0:T(8,128)} %bitcast.617, f32[256,1024]{1,0:T(8,128)S(1)} %get-tuple-element.78, f32[256,1024]{1,0:T(8,128)S(1)} %get-tuple-element.77), kind=kOutput, calls=%fused_computation.38 | convolution fusion | flops 6442975232 | bytes 14680064 | tf_op jit(solution)/shard_map/dot_general | solution.py:66
  308.4 10.5 %convolution_bitcast_fusion = f32[2048,512]{0,1:T(8,128)} fusion(f32[2048,1024]{1,0:T(8,128)} %bitcast.618, f32[256,1024]{1,0:T(8,128)S(1)} %get-tuple-element.80, f32[256,1024]{1,0:T(8,128)S(1)} %get-tuple-element.79), kind=kOutput, calls=%fused_computation.37 | convolution fusion | flops 6442975232 | bytes 14680064 | tf_op jit(solution)/shard_map/dot_general | solution.py:66
  325.1 20.6 %constant_dynamic-slice_fusion.2 = (f32[1,512,512]{1,0,2:T(1,128)}, f32[1,512,512]{1,0,2:T(1,128)}, f32[1,512,512]{1,0,2:T(1,128)S(1)}, f32[1,512,512]{1,0,2:T(1...) fusion(f32[4,512,512]{1,0,2:T(4,128)} %reshape.815, ...), kind=kLoop, calls=%fused_computation.638 | loop fusion | bytes 16777232 | tf_op jit(solution)/shard_map/jit(dynamic_index_in_dim)/dynamic_slice | solution.py:118
  403.6 9.3 %fusion.269 = f32[4,1024,256]{2,1,0:T(8,128)S(1)} fusion(f32[512,1024]{1,0:T(8,128)S(1)} %pad_maximum_fusion.2, f32[4,512,1024]{2,1,0:T(8,128)} %copy-done.1, f32[4,512,1024]{2,1,0:T(8,128)S(1)} %bitcast.620), kind=kOutput, calls=%fused_computation.413 | convolution fusion | flops 6446645248 | bytes 22020096 | tf_op jit(solution)/shard_map/dot_general | solution.py:66
  412.9 10.3 %fusion.270 = f32[4,1024,256]{2,1,0:T(8,128)} fusion(f32[512,1024]{1,0:T(8,128)S(1)} %pad_maximum_fusion.2, f32[4,512,1024]{2,1,0:T(8,128)} %copy-done.1, f32[4,512,1024]{2,1,0:T(8,128)S(1)} %bitcast.620), kind=kOutput, calls=%fused_computation.415 | convolution fusion | flops 6446645248 | bytes 22020096 | tf_op jit(solution)/shard_map/dot_general | solution.py:66
  441.3 27.1 %collective-permute-done.16 = bf16[1040,256]{1,0:T(8,128)(2,1)S(1)} collective-permute-done((bf16[1040,256]{1,0:T(8,128)(2,1)S(1)}, bf16[1040,256]{1,0:T(8,128)(2,1)S(1)}, u32[]{:S(2)}, u32[]{:S(2)}) %collective-permute-start.16) | collective-permute-done | bytes 532512 | tf_op jit(solution)/shard_map/ppermute | solution.py:99
  468.4 34.4 %collective-permute-done.17 = bf16[1040,256]{1,0:T(8,128)(2,1)S(1)} collective-permute-done((bf16[1040,256]{1,0:T(8,128)(2,1)S(1)}, bf16[1040,256]{1,0:T(8,128)(2,1)S(1)}, u32[]{:S(2)}, u32[]{:S(2)}) %collective-permute-start.17) | collective-permute-done | bytes 532512 | tf_op jit(solution)/shard_map/ppermute | solution.py:99
  508.3 17.2 %collective-permute-done.21 = bf16[1040,256]{1,0:T(8,128)(2,1)S(1)} collective-permute-done((bf16[1040,256]{1,0:T(8,128)(2,1)S(1)}, bf16[1040,256]{1,0:T(8,128)(2,1)S(1)}, u32[]{:S(2)}, u32[]{:S(2)}) %collective-permute-start.21) | collective-permute-done | bytes 532512 | tf_op jit(solution)/shard_map/ppermute | solution.py:99
  529.9 12.2 %collective-permute-done.23 = bf16[1024,256]{1,0:T(8,128)(2,1)S(1)} collective-permute-done((bf16[1024,256]{1,0:T(8,128)(2,1)S(1)}, bf16[1024,256]{1,0:T(8,128)(2,1)S(1)}, u32[]{:S(2)}, u32[]{:S(2)}) %collective-permute-start.23) | collective-permute-done | bytes 524320 | tf_op jit(solution)/shard_map/ppermute | solution.py:99
  (222 shorter events, 185.9 us)
Async XLA Ops:
  6.5 140.6 %all-gather.13.cloned.1.call-start = ((), (), s32[]{:S(2)}) async-start(), calls=%async_computation.2 | async-start | bytes 2662400 | tf_op jit(solution)/shard_map/all_gather | solution.py:154
  8.3 15.8 %collective-permute-start.4 = (bf16[1024,256]{1,0:T(8,128)(2,1)S(1)}, bf16[1024,256]{1,0:T(8,128)(2,1)S(1)}, u32[]{:S(2)}, u32[]{:S(2)}) collective-permute-start(bf16[1024,256]{1,0:T(8,128)(2,1)S(1)} %get-tuple-element.87), channel_id=1, source_target_pairs={{0,16},{16,0},{1,17},{17,1},{2,18},{18,2},{3,19},{19,3},{4,20},{20... | collective-permute-start | bytes 1572872 | tf_op jit(solution)/shard_map/ppermute | solution.py:99
  11.3 23.2 %collective-permute-start.5 = (bf16[1024,256]{1,0:T(8,128)(2,1)S(1)}, bf16[1024,256]{1,0:T(8,128)(2,1)S(1)}, u32[]{:S(2)}, u32[]{:S(2)}) collective-permute-start(bf16[1024,256]{1,0:T(8,128)(2,1)S(1)} %get-tuple-element.88), channel_id=1, source_target_pairs={{0,16},{16,0},{1,17},{17,1},{2,18},{18,2},{3,19},{19,3},{4,20},{20... | collective-permute-start | bytes 1572872 | tf_op jit(solution)/shard_map/ppermute | solution.py:99
  36.7 138.7 %all-gather.9.cloned.1.call-start = ((), (), s32[]{:S(2)}) async-start(), calls=%async_computation | async-start | bytes 2662400 | tf_op jit(solution)/shard_map/all_gather | solution.py:154
  41.1 25.1 %collective-permute-start = (bf16[528,1024]{1,0:T(8,128)(2,1)S(1)}, bf16[528,1024]{1,0:T(8,128)(2,1)S(1)}, u32[]{:S(2)}, u32[]{:S(2)}) collective-permute-start(bf16[528,1024]{1,0:T(8,128)(2,1)S(1)} %fusion.72), channel_id=1, source_target_pairs={{0,16},{16,0},{1,17},{17,1},{2,18},{18,2},{3,19},{19,3},{4,20},{20... | collective-permute-start | bytes 3244040 | tf_op jit(solution)/shard_map/ppermute | solution.py:99
  66.2 25.7 %collective-permute-start.1 = (bf16[528,1024]{1,0:T(8,128)(2,1)S(1)}, bf16[528,1024]{1,0:T(8,128)(2,1)}, u32[]{:S(2)}, u32[]{:S(2)}) collective-permute-start(bf16[528,1024]{1,0:T(8,128)(2,1)S(1)} %collective-permute-done), channel_id=1, source_target_pairs={{0,1},{1,2},{2,3},{3,0},{4,5},{5,6},{6,7},{7,4},{8,9},{9,10},{10,1... | collective-permute-start | bytes 3244040 | tf_op jit(solution)/shard_map/ppermute | solution.py:99
  66.2 28.4 %collective-permute-start.2 = (bf16[528,1024]{1,0:T(8,128)(2,1)S(1)}, bf16[528,1024]{1,0:T(8,128)(2,1)}, u32[]{:S(2)}, u32[]{:S(2)}) collective-permute-start(bf16[528,1024]{1,0:T(8,128)(2,1)S(1)} %collective-permute-done), channel_id=1, source_target_pairs={{0,2},{1,3},{2,0},{3,1},{4,6},{5,7},{6,4},{7,5},{8,10},{9,11},{10,... | collective-permute-start | bytes 3244040 | tf_op jit(solution)/shard_map/ppermute | solution.py:99
  67.6 46.8 %collective-permute-start.3 = (bf16[528,1024]{1,0:T(8,128)(2,1)S(1)}, bf16[528,1024]{1,0:T(8,128)(2,1)}, u32[]{:S(2)}, u32[]{:S(2)}) collective-permute-start(bf16[528,1024]{1,0:T(8,128)(2,1)S(1)} %collective-permute-done), channel_id=1, source_target_pairs={{0,3},{1,0},{2,1},{3,2},{4,7},{5,4},{6,5},{7,6},{8,11},{9,8},{10,9... | collective-permute-start | bytes 3244040 | tf_op jit(solution)/shard_map/ppermute | solution.py:99
  69.9 130.0 %all-gather.15.cloned.1.call-start = ((), (), s32[]{:S(2)}) async-start(), calls=%async_computation.3 | async-start | bytes 2785280 | tf_op jit(solution)/shard_map/all_gather | solution.py:157
  163.3 55.9 %all-gather.11.cloned.1.call-start = ((), (), s32[]{:S(2)}) async-start(), calls=%async_computation.1 | async-start | bytes 2785280 | tf_op jit(solution)/shard_map/all_gather | solution.py:157
  243.3 25.2 %collective-permute-start.6 = (bf16[272,1024]{1,0:T(8,128)(2,1)S(1)}, bf16[272,1024]{1,0:T(8,128)(2,1)S(1)}, u32[]{:S(2)}, u32[]{:S(2)}) collective-permute-start(bf16[272,1024]{1,0:T(8,128)(2,1)S(1)} %fusion.355), channel_id=1, source_target_pairs={{0,16},{16,0},{1,17},{17,1},{2,18},{18,2},{3,19},{19,3},{4,20},{20... | collective-permute-start | bytes 1671176 | tf_op jit(solution)/shard_map/ppermute | solution.py:99
  271.5 15.7 %collective-permute-start.7 = (bf16[272,1024]{1,0:T(8,128)(2,1)S(1)}, bf16[272,1024]{1,0:T(8,128)(2,1)}, u32[]{:S(2)}, u32[]{:S(2)}) collective-permute-start(bf16[272,1024]{1,0:T(8,128)(2,1)S(1)} %fusion.356), channel_id=1, source_target_pairs={{0,16},{16,0},{1,17},{17,1},{2,18},{18,2},{3,19},{19,3},{4,20},{20... | collective-permute-start | bytes 1671176 | tf_op jit(solution)/shard_map/ppermute | solution.py:99
  273.4 32.8 %collective-permute-start.12 = (bf16[272,1024]{1,0:T(8,128)(2,1)S(1)}, bf16[272,1024]{1,0:T(8,128)(2,1)}, u32[]{:S(2)}, u32[]{:S(2)}) collective-permute-start(bf16[272,1024]{1,0:T(8,128)(2,1)S(1)} %fusion.358), channel_id=1, source_target_pairs={{0,16},{16,0},{1,17},{17,1},{2,18},{18,2},{3,19},{19,3},{4,20},{20... | collective-permute-start | bytes 1671176 | tf_op jit(solution)/shard_map/ppermute | solution.py:99
  351.6 36.1 %collective-permute-start.8 = (bf16[528,512]{1,0:T(8,128)(2,1)}, bf16[528,512]{1,0:T(8,128)(2,1)}, u32[]{:S(2)}, u32[]{:S(2)}) collective-permute-start(bf16[528,512]{1,0:T(8,128)(2,1)} %fusion.359), channel_id=1, source_target_pairs={{0,1},{1,2},{2,3},{3,0},{4,5},{5,6},{6,7},{7,4},{8,9},{9,10},{10,1... | collective-permute-start | bytes 1622024 | tf_op jit(solution)/shard_map/ppermute | solution.py:99
  357.6 32.3 %collective-permute-start.9 = (bf16[528,512]{1,0:T(8,128)(2,1)}, bf16[528,512]{1,0:T(8,128)(2,1)}, u32[]{:S(2)}, u32[]{:S(2)}) collective-permute-start(bf16[528,512]{1,0:T(8,128)(2,1)} %fusion.360), channel_id=1, source_target_pairs={{0,2},{1,3},{2,0},{3,1},{4,6},{5,7},{6,4},{7,5},{8,10},{9,11},{10,... | collective-permute-start | bytes 1622024 | tf_op jit(solution)/shard_map/ppermute | solution.py:99
  363.9 26.7 %collective-permute-start.10 = (bf16[528,512]{1,0:T(8,128)(2,1)}, bf16[528,512]{1,0:T(8,128)(2,1)}, u32[]{:S(2)}, u32[]{:S(2)}) collective-permute-start(bf16[528,512]{1,0:T(8,128)(2,1)} %fusion.361), channel_id=1, source_target_pairs={{0,3},{1,0},{2,1},{3,2},{4,7},{5,4},{6,5},{7,6},{8,11},{9,8},{10,9... | collective-permute-start | bytes 1622024 | tf_op jit(solution)/shard_map/ppermute | solution.py:99
  375.0 16.4 %collective-permute-start.13 = (bf16[528,512]{1,0:T(8,128)(2,1)}, bf16[528,512]{1,0:T(8,128)(2,1)}, u32[]{:S(2)}, u32[]{:S(2)}) collective-permute-start(bf16[528,512]{1,0:T(8,128)(2,1)} %fusion.362), channel_id=1, source_target_pairs={{0,1},{1,2},{2,3},{3,0},{4,5},{5,6},{6,7},{7,4},{8,9},{9,10},{10,1... | collective-permute-start | bytes 1622024 | tf_op jit(solution)/shard_map/ppermute | solution.py:99
  428.5 78.5 %collective-permute-start.19 = (bf16[1040,256]{1,0:T(8,128)(2,1)}, bf16[1040,256]{1,0:T(8,128)(2,1)}, u32[]{:S(2)}, u32[]{:S(2)}) collective-permute-start(bf16[1040,256]{1,0:T(8,128)(2,1)} %fusion.370), channel_id=1, source_target_pairs={{0,4},{4,8},{8,12},{12,0},{1,5},{5,9},{9,13},{13,1},{2,6},{6,10},{... | collective-permute-start | bytes 1597448 | tf_op jit(solution)/shard_map/ppermute | solution.py:99
  431.2 76.4 %collective-permute-start.20 = (bf16[1040,256]{1,0:T(8,128)(2,1)}, bf16[1040,256]{1,0:T(8,128)(2,1)}, u32[]{:S(2)}, u32[]{:S(2)}) collective-permute-start(bf16[1040,256]{1,0:T(8,128)(2,1)} %fusion.371), channel_id=1, source_target_pairs={{0,8},{4,12},{8,0},{12,4},{1,9},{5,13},{9,1},{13,5},{2,10},{6,14},... | collective-permute-start | bytes 1597448 | tf_op jit(solution)/shard_map/ppermute | solution.py:99
  437.1 31.2 %collective-permute-start.16 = (bf16[1040,256]{1,0:T(8,128)(2,1)S(1)}, bf16[1040,256]{1,0:T(8,128)(2,1)S(1)}, u32[]{:S(2)}, u32[]{:S(2)}) collective-permute-start(bf16[1040,256]{1,0:T(8,128)(2,1)S(1)} %fusion.367), channel_id=1, source_target_pairs={{0,4},{4,8},{8,12},{12,0},{1,5},{5,9},{9,13},{13,1},{2,6},{6,10},{... | collective-permute-start | bytes 1597448 | tf_op jit(solution)/shard_map/ppermute | solution.py:99
  437.5 65.2 %collective-permute-start.17 = (bf16[1040,256]{1,0:T(8,128)(2,1)S(1)}, bf16[1040,256]{1,0:T(8,128)(2,1)S(1)}, u32[]{:S(2)}, u32[]{:S(2)}) collective-permute-start(bf16[1040,256]{1,0:T(8,128)(2,1)S(1)} %fusion.368), channel_id=1, source_target_pairs={{0,8},{4,12},{8,0},{12,4},{1,9},{5,13},{9,1},{13,5},{2,10},{6,14},... | collective-permute-start | bytes 1597448 | tf_op jit(solution)/shard_map/ppermute | solution.py:99
  439.4 63.4 %collective-permute-start.18 = (bf16[1040,256]{1,0:T(8,128)(2,1)S(1)}, bf16[1040,256]{1,0:T(8,128)(2,1)S(1)}, u32[]{:S(2)}, u32[]{:S(2)}) collective-permute-start(bf16[1040,256]{1,0:T(8,128)(2,1)S(1)} %fusion.369), channel_id=1, source_target_pairs={{0,12},{4,0},{8,4},{12,8},{1,13},{5,1},{9,5},{13,9},{2,14},{6,2},{... | collective-permute-start | bytes 1597448 | tf_op jit(solution)/shard_map/ppermute | solution.py:99
  468.4 57.2 %collective-permute-start.21 = (bf16[1040,256]{1,0:T(8,128)(2,1)S(1)}, bf16[1040,256]{1,0:T(8,128)(2,1)S(1)}, u32[]{:S(2)}, u32[]{:S(2)}) collective-permute-start(bf16[1040,256]{1,0:T(8,128)(2,1)S(1)} %fusion.372), channel_id=1, source_target_pairs={{0,12},{4,0},{8,4},{12,8},{1,13},{5,1},{9,5},{13,9},{2,14},{6,2},{... | collective-permute-start | bytes 1597448 | tf_op jit(solution)/shard_map/ppermute | solution.py:99
  505.2 24.6 %collective-permute-start.22 = (bf16[1024,256]{1,0:T(8,128)(2,1)S(1)}, bf16[1024,256]{1,0:T(8,128)(2,1)S(1)}, u32[]{:S(2)}, u32[]{:S(2)}) collective-permute-start(bf16[1024,256]{1,0:T(8,128)(2,1)S(1)} %fusion.259), channel_id=1, source_target_pairs={{0,16},{16,0},{1,17},{17,1},{2,18},{18,2},{3,19},{19,3},{4,20},{20... | collective-permute-start | bytes 1572872 | tf_op jit(solution)/shard_map/ppermute | solution.py:99
  (18 other events, 135.1 us)
Sparse Core Ops, SparseCore 0:
  36.8 48.0 all-gather.12
  86.4 45.2 all-gather.8
  163.4 27.4 all-gather.14
  192.3 26.8 all-gather.10

commit v2 on v1

--- a/solution.py
+++ b/solution.py
@@ -53,7 +53,6 @@
 
 
 CHUNKS_IN = 2
-CHUNKS_MID = 2
 CHUNKS_OUT = 2
 GROUP = 128
 SPAN = 240.0
@@ -110,17 +109,33 @@
     )
 
 
-def scatter_blocks(blocks, axis, finish):
+def after(later, earlier):
+    later, earlier = lax.optimization_barrier((later, earlier))
+    return later, earlier
+
+
+def order_of(n):
+    return sorted(range(1, n), key=lambda s: -min(s, n - s)) + [0]
+
+
+def scatter_products(blocks, other, axis):
     n = lax.axis_size(axis)
     i = lax.axis_index(axis)
-    sent = []
-    for step in range(1, n):
+    sent, own = [], None
+    for step in order_of(n):
         block = lax.dynamic_index_in_dim(blocks, lax.rem(i + step, n), 0, False)
-        sent.append(shift(encode(block), axis, step))
-    total = lax.dynamic_index_in_dim(blocks, i, 0, False)
+        term = matmul(block, other, contract_last)
+        if step == 0:
+            own = term
+        else:
+            sent.append(shift(encode(term), axis, step))
+    return own, sent
+
+
+def add_up(own, sent):
     for got in sent:
-        total = total + decode(got)
-    return finish(total)
+        own = own + decode(got)
+    return own
 
 
 def pair_body(grads, left_basis, right_basis, eigen_left, eigen_right):
@@ -128,63 +143,64 @@
     col = lax.axis_index("col")
     cols = lax.axis_size("col")
     blocks, tall, wide = left_basis.shape
-    columns = right_basis.shape[2]
+    lines, columns = right_basis.shape[1:]
 
     grad = grads[0]
     keep, give = half(grad, me, 1), half(grad, 1 - me, 1)
     width = keep.shape[1] // CHUNKS_IN
+    got = [
+        shift(give[:, c * width : (c + 1) * width], "rep", 1) for c in range(CHUNKS_IN)
+    ]
     coded = []
     for c in range(CHUNKS_IN):
-        at = slice(c * width, (c + 1) * width)
-        got = shift(give[:, at], "rep", 1)
-        coded.append(encode(keep[:, at].astype(jnp.float32) + got.astype(jnp.float32)))
-
-    share = lax.dynamic_index_in_dim(left_basis, col, 0, False)
-    share = shift(encode(share), "rep", 1)
-    shares = [share] + [shift(share, "col", s) for s in range(1, cols)]
-    rolled = jnp.stack([decode(s) for s in shares])
-    place = lax.rem(col - jnp.arange(blocks) + cols, cols)
-    other = jnp.take(rolled, place, axis=0, mode="clip")
-    left = ordered(left_basis, other, me, 1).reshape(-1, wide)
-
-    right = right_basis
-    lines = right.shape[1]
-    rotated = 0.0
+        part, arrived = keep[:, c * width : (c + 1) * width], got[c]
+        if c > 0:
+            arrived, coded[c - 1] = after(arrived, coded[c - 1])
+        coded.append(encode(part.astype(jnp.float32) + arrived.astype(jnp.float32)))
+
+    share = shift(
+        encode(lax.dynamic_index_in_dim(left_basis, col, 0, False)), "rep", 1
+    )
+    left = jnp.zeros((blocks, 2 * tall, wide), jnp.float32)
+    left = lax.dynamic_update_slice(left, left_basis, (0, me * tall, 0))
+    for step in range(cols):
+        piece = share if step == 0 else shift(share, "col", step)
+        place = lax.rem(col - step + cols, cols)
+        left = lax.dynamic_update_slice(
+            left, decode(piece)[None], (place, (1 - me) * tall, 0)
+        )
+    left_flat = left.reshape(-1, wide)
+
+    keep = give = 0.0
+    w = lines // CHUNKS_IN
     for c in range(CHUNKS_IN):
         stacked = lax.all_gather(coded[c], "row", axis=0)
         stacked = jnp.concatenate([decode(s) for s in stacked], axis=0)
-        part = encode(matmul(stacked, left, contract_first))
+        part = encode(matmul(stacked, left_flat, contract_first))
         gathered = lax.all_gather(part, "col", axis=0)
-        gathered = jnp.concatenate([decode(s) for s in gathered], axis=0)
-        w = lines // CHUNKS_IN
-        r = right[:, c * w : (c + 1) * w].reshape(-1, columns)
-        rotated = rotated + matmul(gathered, r, contract_first)
+        r = right_basis[:, c * w : (c + 1) * w].reshape(-1, columns)
+        for_peer = [decode(half(s, 1 - me, 1)) for s in gathered]
+        give = give + matmul(jnp.concatenate(for_peer, axis=0), r, contract_first)
+        for_me = [decode(half(s, me, 1)) for s in gathered]
+        keep = keep + matmul(jnp.concatenate(for_me, axis=0), r, contract_first)
 
     eigen = eigen_left[:, None] + eigen_right[None, :] + epsilon
-    eigen = half(eigen, me, 0)
-    keep, give = half(rotated, me, 0), half(rotated, 1 - me, 0)
-    right_flat = right.reshape(-1, columns)
-    high = keep.shape[0] // CHUNKS_MID
-    backs = []
-    for c in range(CHUNKS_MID):
-        at = slice(c * high, (c + 1) * high)
-        got = shift(encode(give[at]), "rep", 1)
-        mine = (keep[at] + decode(got)) / eigen[at]
-        peer = decode(shift(encode(mine), "rep", 1))
-        scaled = ordered(mine, peer, me, 0)
-        back = matmul(right_flat, scaled, contract_last)
-        back = back.reshape(cols, -1, back.shape[1])
-        backs.append(scatter_blocks(back, "col", lambda t: t))
-    back = jnp.concatenate(
-        [b[:, s * high : (s + 1) * high] for s in range(2) for b in backs], axis=1
-    )
+    mine = (keep + decode(shift(encode(give), "rep", 1))) / half(eigen, me, 0)
+    peer = decode(shift(encode(mine), "rep", 1))
+    first = scatter_products(right_basis, mine, "col")
+    second = scatter_products(right_basis, peer, "col")
+    back = ordered(add_up(*first), add_up(*second), me, 1)
 
     narrow = back.shape[0] // CHUNKS_OUT
+    pending = [
+        scatter_products(left, back[c * narrow : (c + 1) * narrow], "row")
+        for c in range(CHUNKS_OUT)
+    ]
     mine, peer = [], []
-    for c in range(CHUNKS_OUT):
-        out = matmul(left, back[c * narrow : (c + 1) * narrow], contract_last)
-        out = out.reshape(blocks, -1, narrow)
-        done = scatter_blocks(out, "row", lambda t: t.astype(jnp.bfloat16))
+    for c, (own, sent) in enumerate(pending):
+        if c > 0:
+            own, mine[c - 1] = after(own, mine[c - 1])
+        done = add_up(own, sent).astype(jnp.bfloat16)
         mine.append(done)
         peer.append(shift(done, "rep", 1))
     return ordered(

time: 562 us -> 549 us (0.977)
  the two profiles are of different devices: /device:TPU:0 before, /device:TPU:16 now
where the time goes in v2:
time: 549 us; the launch traced here: 541 us
  waiting for transfers between devices  232 us (42%)
  matrix products  106 us (19%)
  local copies, waits for them, and re-layouts  90.1 us (16%)
  other arithmetic  72 us (13%)
  starting transfers between devices  26.9 us (5%)
  between operations  14.8 us (3%)
    ppermute x22, waiting for transfers between devices, shift(): return lax.ppermute(x, axis, [(s, (s + step) % n) for s in range(n)])  209 us
    dot_general x22, matrix products, matmul(): lax.dot_general(a, b, dims, precision=lax.Precision.HIGH, preferred_eleme...  106 us
    ppermute x22, starting transfers between devices, shift(): return lax.ppermute(x, axis, [(s, (s + step) % n) for s in range(n)])  26 us
    all_gather x2, waiting for transfers between devices, pair_body(): gathered = lax.all_gather(part, 'col', axis=0)  22.8 us
    reshape x6, local copies, waits for them, and re-layouts, encode(): top = jnp.max(jnp.abs(x).reshape(groups, GROUP, columns), axis=1)  15.3 us
    convert_element_type x19, other arithmetic, encode(): code = jnp.where(x < 0, -power, power).astype(jnp.bfloat16)  14.3 us
    unnamed x47, local copies, waits for them, and re-layouts  12.4 us
    reduce_max x9, other arithmetic, encode(): top = jnp.max(jnp.abs(x).reshape(groups, GROUP, columns), axis=1)  11.6 us
  transfers between devices with their start and end apart: 26, of which 14 were waited for; matrix products, arithmetic and copies ran while one was open for 33% of the time, Pallas kernels for 0%

profile of v2, /device:TPU:16, one launch (start us, length us, event | category | flops | bytes accessed | tf_op | source)
XLA Modules:
  0.0 541.5 jit_solution(16994976311000816927)
XLA Ops:
  10.4 12.8 %collective-permute-done.5 = bf16[1024,256]{1,0:T(8,128)(2,1)S(1)} collective-permute-done((bf16[1024,256]{1,0:T(8,128)(2,1)S(1)}, bf16[1024,256]{1,0:T(8,128)(2,1)S(1)}, u32[]{:S(2)}, u32[]{:S(2)}) %collective-permute-start.5) | collective-permute-done | bytes 524320 | tf_op jit(solution)/shard_map/ppermute | solution.py:98
  24.6 8.6 %collective-permute-done.4 = bf16[1024,256]{1,0:T(8,128)(2,1)S(1)} collective-permute-done((bf16[1024,256]{1,0:T(8,128)(2,1)S(1)}, bf16[1024,256]{1,0:T(8,128)(2,1)S(1)}, u32[]{:S(2)}, u32[]{:S(2)}) %collective-permute-start.4) | collective-permute-done | bytes 524320 | tf_op jit(solution)/shard_map/ppermute | solution.py:98
  40.0 7.9 %broadcast_in_dim.132 = f32[4,1024,1024]{2,1,0:T(8,128)} broadcast(f32[]{:T(128)} %constant.185.clone.1), dimensions={} | broadcast | bytes 16777220 | tf_op jit(solution)/shard_map/broadcast_in_dim | solution.py:164
  47.9 8.3 %constant_dynamic-update-slice_fusion = f32[4,1024,1024]{2,1,0:T(8,128)} fusion(f32[4,1024,1024]{2,1,0:T(8,128)} %broadcast_in_dim.132, f32[4,512,1024]{2,1,0:T(8,128)} %param.6, s32[]{:T(128)S(6)} %select_n.284), kind=kLoop, calls=%fused_computation.731 | loop fusion | bytes 16777220 | tf_op jit(solution)/shard_map/dynamic_update_slice | solution.py:165
  56.2 7.0 %collective-permute-done = bf16[528,1024]{1,0:T(8,128)(2,1)S(1)} collective-permute-done((bf16[528,1024]{1,0:T(8,128)(2,1)S(1)}, bf16[528,1024]{1,0:T(8,128)(2,1)S(1)}, u32[]{:S(2)}, u32[]{:S(2)}) %collective-permute-start) | collective-permute-done | bytes 1081376 | tf_op jit(solution)/shard_map/ppermute | solution.py:98
  70.3 18.3 %collective-permute-done.1 = bf16[528,1024]{1,0:T(8,128)(2,1)} collective-permute-done((bf16[528,1024]{1,0:T(8,128)(2,1)S(1)}, bf16[528,1024]{1,0:T(8,128)(2,1)}, u32[]{:S(2)}, u32[]{:S(2)}) %collective-permute-start.1) | collective-permute-done | bytes 1081376 | tf_op jit(solution)/shard_map/ppermute | solution.py:98
  90.2 21.4 %collective-permute-done.3 = bf16[528,1024]{1,0:T(8,128)(2,1)} collective-permute-done((bf16[528,1024]{1,0:T(8,128)(2,1)S(1)}, bf16[528,1024]{1,0:T(8,128)(2,1)}, u32[]{:S(2)}, u32[]{:S(2)}) %collective-permute-start.3) | collective-permute-done | bytes 1081376 | tf_op jit(solution)/shard_map/ppermute | solution.py:98
  125.3 11.2 %bitcast_reduce_fusion.10 = (f32[2,1024]{1,0:T(2,128)S(1)}, f32[256,1024]{1,0:T(8,128)S(1)}) fusion(f32[4096,1024]{1,0:T(8,128)} %bitcast.35, f32[1024,256]{1,0:T(8,128)S(1)} %get-tuple-element.34, f32[1024,256]{1,0:T(8,128)S(1)} %get-tuple-element.35, f32[1024,256]{1,0:T(8,128)S(1)} %get-tuple-element.36, f32[1024,256]{1,0:T(8,128)S(1)} %get-tuple-element.33), kind=kOutput, calls=%fused_computation.464 | convolution fusion | flops 6446118912 | bytes 22028288 | tf_op jit(solution)/shard_map/dot_general | solution.py:65
  141.9 11.2 %bitcast_reduce_fusion.8 = (f32[2,1024]{1,0:T(2,128)S(1)}, f32[256,1024]{1,0:T(8,128)S(1)}) fusion(f32[4096,1024]{1,0:T(8,128)} %bitcast.35, f32[1024,256]{1,0:T(8,128)S(1)} %get-tuple-element.26, f32[1024,256]{1,0:T(8,128)S(1)} %get-tuple-element.27, f32[1024,256]{1,0:T(8,128)S(1)} %get-tuple-element.28, f32[1024,256]{1,0:T(8,128)S(1)} %get-tuple-element.25), kind=kOutput, calls=%fused_computation.454 | convolution fusion | flops 6446118912 | bytes 22028288 | tf_op jit(solution)/shard_map/dot_general | solution.py:65
  154.5 8.5 %fusion.527 = (f32[4,256,1024]{2,1,0:T(8,128)}, f32[4,256,1024]{2,1,0:T(8,128)}) fusion(f32[4,512,1024]{2,1,0:T(8,128)} %param.7), kind=kLoop, calls=%fused_computation.788 | loop fusion | bytes 16777216 | tf_op jit(solution)/shard_map/slice | solution.py:181
  165.1 22.7 %all-gather.15.cloned.1.call-done = bf16[1088,1024]{1,0:T(8,128)(2,1)} async-done(((bf16[272,1024]{1,0:T(8,128)(2,1)}), bf16[1088,1024]{1,0:T(8,128)(2,1)}) %all-gather.15.cloned.1.call-update) | async-done | bytes 2228240 | tf_op jit(solution)/shard_map/all_gather | solution.py:180
  208.0 19.2 %collective-permute-done.6 = bf16[528,1024]{1,0:T(8,128)(2,1)S(1)} collective-permute-done((bf16[528,1024]{1,0:T(8,128)(2,1)S(1)}, bf16[528,1024]{1,0:T(8,128)(2,1)S(1)}, u32[]{:S(2)}, u32[]{:S(2)}) %collective-permute-start.6) | collective-permute-done | bytes 1081376 | tf_op jit(solution)/shard_map/ppermute | solution.py:98
  227.2 4.8 bitcast_reduce_fusion
  278.2 19.3 %collective-permute-done.10 = bf16[528,1024]{1,0:T(8,128)(2,1)} collective-permute-done((bf16[528,1024]{1,0:T(8,128)(2,1)}, bf16[528,1024]{1,0:T(8,128)(2,1)}, u32[]{:S(2)}, u32[]{:S(2)}) %collective-permute-start.10) | collective-permute-done | bytes 1081376 | tf_op jit(solution)/shard_map/ppermute | solution.py:98
  300.1 5.6 %fusion.536 = (f32[512,512]{0,1:T(8,128)}, f32[512,512]{0,1:T(8,128)}) fusion(f32[512,1024]{1,0:T(8,128)S(1)} %negate_select_fusion, f32[4,512,1024]{2,1,0:T(8,128)} %param.7, s32[]{:T(128)S(6)} %select_n.291), kind=kOutput, calls=%fused_computation.797 | convolution fusion | flops 1610874880 | bytes 6291460 | tf_op jit(solution)/shard_map/dot_general | solution.py:65
  305.7 4.9 fusion.535
  310.6 4.5 fusion.534
  370.8 4.4 fusion.160
  377.1 4.7 broadcast_select_fusion.3
  419.5 57.0 %collective-permute-done.14 = bf16[1040,256]{1,0:T(8,128)(2,1)S(1)} collective-permute-done((bf16[1040,256]{1,0:T(8,128)(2,1)S(1)}, bf16[1040,256]{1,0:T(8,128)(2,1)S(1)}, u32[]{:S(2)}, u32[]{:S(2)}) %collective-permute-start.14) | collective-permute-done | bytes 532512 | tf_op jit(solution)/shard_map/ppermute | solution.py:98
  478.9 23.3 %collective-permute-done.15 = bf16[1040,256]{1,0:T(8,128)(2,1)S(1)} collective-permute-done((bf16[1040,256]{1,0:T(8,128)(2,1)S(1)}, bf16[1040,256]{1,0:T(8,128)(2,1)S(1)}, u32[]{:S(2)}, u32[]{:S(2)}) %collective-permute-start.15) | collective-permute-done | bytes 532512 | tf_op jit(solution)/shard_map/ppermute | solution.py:98
  502.2 5.0 fusion.287
  510.6 11.4 %collective-permute-done.20 = bf16[1024,256]{1,0:T(8,128)(2,1)S(1)} collective-permute-done((bf16[1024,256]{1,0:T(8,128)(2,1)S(1)}, bf16[1024,256]{1,0:T(8,128)(2,1)S(1)}, u32[]{:S(2)}, u32[]{:S(2)}) %collective-permute-start.20) | collective-permute-done | bytes 524320 | tf_op jit(solution)/shard_map/ppermute | solution.py:98
  522.1 10.3 %collective-permute-done.21 = bf16[1024,256]{1,0:T(8,128)(2,1)S(1)} collective-permute-done((bf16[1024,256]{1,0:T(8,128)(2,1)S(1)}, bf16[1024,256]{1,0:T(8,128)(2,1)S(1)}, u32[]{:S(2)}, u32[]{:S(2)}) %collective-permute-start.21) | collective-permute-done | bytes 524320 | tf_op jit(solution)/shard_map/ppermute | solution.py:98
  (297 shorter events, 214.2 us)
Async XLA Ops:
  6.5 115.2 %all-gather.9.cloned.1.call-start = ((), (), s32[]{:S(2)}) async-start(), calls=%async_computation | async-start | bytes 2662400 | tf_op jit(solution)/shard_map/all_gather | solution.py:177
  8.3 14.9 %collective-permute-start.5 = (bf16[1024,256]{1,0:T(8,128)(2,1)S(1)}, bf16[1024,256]{1,0:T(8,128)(2,1)S(1)}, u32[]{:S(2)}, u32[]{:S(2)}) collective-permute-start(bf16[1024,256]{1,0:T(8,128)(2,1)S(1)} %get-tuple-element.49), channel_id=1, source_target_pairs={{0,16},{16,0},{1,17},{17,1},{2,18},{18,2},{3,19},{19,3},{4,20},{20... | collective-permute-start | bytes 1572872 | tf_op jit(solution)/shard_map/ppermute | solution.py:98
  9.9 23.4 %collective-permute-start.4 = (bf16[1024,256]{1,0:T(8,128)(2,1)S(1)}, bf16[1024,256]{1,0:T(8,128)(2,1)S(1)}, u32[]{:S(2)}, u32[]{:S(2)}) collective-permute-start(bf16[1024,256]{1,0:T(8,128)(2,1)S(1)} %get-tuple-element.50), channel_id=1, source_target_pairs={{0,16},{16,0},{1,17},{17,1},{2,18},{18,2},{3,19},{19,3},{4,20},{20... | collective-permute-start | bytes 1572872 | tf_op jit(solution)/shard_map/ppermute | solution.py:98
  33.3 105.0 %all-gather.13.cloned.1.call-start = ((), (), s32[]{:S(2)}) async-start(), calls=%async_computation.2 | async-start | bytes 2662400 | tf_op jit(solution)/shard_map/all_gather | solution.py:177
  38.4 24.8 %collective-permute-start = (bf16[528,1024]{1,0:T(8,128)(2,1)S(1)}, bf16[528,1024]{1,0:T(8,128)(2,1)S(1)}, u32[]{:S(2)}, u32[]{:S(2)}) collective-permute-start(bf16[528,1024]{1,0:T(8,128)(2,1)S(1)} %fusion.174), channel_id=1, source_target_pairs={{0,16},{16,0},{1,17},{17,1},{2,18},{18,2},{3,19},{19,3},{4,20},{20... | collective-permute-start | bytes 3244040 | tf_op jit(solution)/shard_map/ppermute | solution.py:98
  63.2 25.5 %collective-permute-start.1 = (bf16[528,1024]{1,0:T(8,128)(2,1)S(1)}, bf16[528,1024]{1,0:T(8,128)(2,1)}, u32[]{:S(2)}, u32[]{:S(2)}) collective-permute-start(bf16[528,1024]{1,0:T(8,128)(2,1)S(1)} %collective-permute-done), channel_id=1, source_target_pairs={{0,1},{1,2},{2,3},{3,0},{4,5},{5,6},{6,7},{7,4},{8,9},{9,10},{10,1... | collective-permute-start | bytes 3244040 | tf_op jit(solution)/shard_map/ppermute | solution.py:98
  63.4 26.8 %collective-permute-start.2 = (bf16[528,1024]{1,0:T(8,128)(2,1)S(1)}, bf16[528,1024]{1,0:T(8,128)(2,1)S(1)}, u32[]{:S(2)}, u32[]{:S(2)}) collective-permute-start(bf16[528,1024]{1,0:T(8,128)(2,1)S(1)} %collective-permute-done), channel_id=1, source_target_pairs={{0,2},{1,3},{2,0},{3,1},{4,6},{5,7},{6,4},{7,5},{8,10},{9,11},{10,... | collective-permute-start | bytes 3244040 | tf_op jit(solution)/shard_map/ppermute | solution.py:98
  65.4 46.2 %collective-permute-start.3 = (bf16[528,1024]{1,0:T(8,128)(2,1)S(1)}, bf16[528,1024]{1,0:T(8,128)(2,1)}, u32[]{:S(2)}, u32[]{:S(2)}) collective-permute-start(bf16[528,1024]{1,0:T(8,128)(2,1)S(1)} %collective-permute-done), channel_id=1, source_target_pairs={{0,3},{1,0},{2,1},{3,2},{4,7},{5,4},{6,5},{7,6},{8,11},{9,8},{10,9... | collective-permute-start | bytes 3244040 | tf_op jit(solution)/shard_map/ppermute | solution.py:98
  67.7 95.3 %all-gather.11.cloned.1.call-start = ((), (), s32[]{:S(2)}) async-start(), calls=%async_computation.1 | async-start | bytes 2785280 | tf_op jit(solution)/shard_map/all_gather | solution.py:180
  137.7 50.1 %all-gather.15.cloned.1.call-start = ((), (), s32[]{:S(2)}) async-start(), calls=%async_computation.3 | async-start | bytes 2785280 | tf_op jit(solution)/shard_map/all_gather | solution.py:180
  201.0 26.2 %collective-permute-start.6 = (bf16[528,1024]{1,0:T(8,128)(2,1)S(1)}, bf16[528,1024]{1,0:T(8,128)(2,1)S(1)}, u32[]{:S(2)}, u32[]{:S(2)}) collective-permute-start(bf16[528,1024]{1,0:T(8,128)(2,1)S(1)} %fusion.175), channel_id=1, source_target_pairs={{0,16},{16,0},{1,17},{17,1},{2,18},{18,2},{3,19},{19,3},{4,20},{20... | collective-permute-start | bytes 3244040 | tf_op jit(solution)/shard_map/ppermute | solution.py:98
  252.8 23.9 %collective-permute-start.7 = (bf16[528,512]{1,0:T(8,128)(2,1)}, bf16[528,512]{1,0:T(8,128)(2,1)}, u32[]{:S(2)}, u32[]{:S(2)}) collective-permute-start(bf16[528,512]{1,0:T(8,128)(2,1)} %copy.95), channel_id=1, source_target_pairs={{0,2},{1,3},{2,0},{3,1},{4,6},{5,7},{6,4},{7,5},{8,10},{9,11},{10,... | collective-permute-start | bytes 1622024 | tf_op jit(solution)/shard_map/ppermute | solution.py:98
  271.0 26.5 %collective-permute-start.10 = (bf16[528,1024]{1,0:T(8,128)(2,1)}, bf16[528,1024]{1,0:T(8,128)(2,1)}, u32[]{:S(2)}, u32[]{:S(2)}) collective-permute-start(bf16[528,1024]{1,0:T(8,128)(2,1)} %fusion.176), channel_id=1, source_target_pairs={{0,16},{16,0},{1,17},{17,1},{2,18},{18,2},{3,19},{19,3},{4,20},{20... | collective-permute-start | bytes 3244040 | tf_op jit(solution)/shard_map/ppermute | solution.py:98
  274.9 73.5 %collective-permute-start.9 = (bf16[528,512]{1,0:T(8,128)(2,1)}, bf16[528,512]{1,0:T(8,128)(2,1)}, u32[]{:S(2)}, u32[]{:S(2)}) collective-permute-start(bf16[528,512]{1,0:T(8,128)(2,1)} %copy.111), channel_id=1, source_target_pairs={{0,3},{1,0},{2,1},{3,2},{4,7},{5,4},{6,5},{7,6},{8,11},{9,8},{10,9... | collective-permute-start | bytes 1622024 | tf_op jit(solution)/shard_map/ppermute | solution.py:98
  326.4 29.4 %collective-permute-start.13 = (bf16[528,512]{1,0:T(8,128)(2,1)}, bf16[528,512]{1,0:T(8,128)(2,1)}, u32[]{:S(2)}, u32[]{:S(2)}) collective-permute-start(bf16[528,512]{1,0:T(8,128)(2,1)} %copy.135), channel_id=1, source_target_pairs={{0,3},{1,0},{2,1},{3,2},{4,7},{5,4},{6,5},{7,6},{8,11},{9,8},{10,9... | collective-permute-start | bytes 1622024 | tf_op jit(solution)/shard_map/ppermute | solution.py:98
  338.9 20.6 %collective-permute-start.12 = (bf16[528,512]{1,0:T(8,128)(2,1)}, bf16[528,512]{1,0:T(8,128)(2,1)}, u32[]{:S(2)}, u32[]{:S(2)}) collective-permute-start(bf16[528,512]{1,0:T(8,128)(2,1)} %copy.127), channel_id=1, source_target_pairs={{0,1},{1,2},{2,3},{3,0},{4,5},{5,6},{6,7},{7,4},{8,9},{9,10},{10,1... | collective-permute-start | bytes 1622024 | tf_op jit(solution)/shard_map/ppermute | solution.py:98
  347.3 15.9 %collective-permute-start.11 = (bf16[528,512]{1,0:T(8,128)(2,1)}, bf16[528,512]{1,0:T(8,128)(2,1)}, u32[]{:S(2)}, u32[]{:S(2)}) collective-permute-start(bf16[528,512]{1,0:T(8,128)(2,1)} %copy.119), channel_id=1, source_target_pairs={{0,2},{1,3},{2,0},{3,1},{4,6},{5,7},{6,4},{7,5},{8,10},{9,11},{10,... | collective-permute-start | bytes 1622024 | tf_op jit(solution)/shard_map/ppermute | solution.py:98
  406.5 102.2 %collective-permute-start.17 = (bf16[1040,256]{1,0:T(8,128)(2,1)S(1)}, bf16[1040,256]{1,0:T(8,128)(2,1)S(1)}, u32[]{:S(2)}, u32[]{:S(2)}) collective-permute-start(bf16[1040,256]{1,0:T(8,128)(2,1)S(1)} %fusion.369), channel_id=1, source_target_pairs={{0,8},{4,12},{8,0},{12,4},{1,9},{5,13},{9,1},{13,5},{2,10},{6,14},... | collective-permute-start | bytes 1597448 | tf_op jit(solution)/shard_map/ppermute | solution.py:98
  407.6 101.2 %collective-permute-start.18 = (bf16[1040,256]{1,0:T(8,128)(2,1)S(1)}, bf16[1040,256]{1,0:T(8,128)(2,1)S(1)}, u32[]{:S(2)}, u32[]{:S(2)}) collective-permute-start(bf16[1040,256]{1,0:T(8,128)(2,1)S(1)} %fusion.370), channel_id=1, source_target_pairs={{0,4},{4,8},{8,12},{12,0},{1,5},{5,9},{9,13},{13,1},{2,6},{6,10},{... | collective-permute-start | bytes 1597448 | tf_op jit(solution)/shard_map/ppermute | solution.py:98
  413.7 62.8 %collective-permute-start.14 = (bf16[1040,256]{1,0:T(8,128)(2,1)S(1)}, bf16[1040,256]{1,0:T(8,128)(2,1)S(1)}, u32[]{:S(2)}, u32[]{:S(2)}) collective-permute-start(bf16[1040,256]{1,0:T(8,128)(2,1)S(1)} %fusion.366), channel_id=1, source_target_pairs={{0,8},{4,12},{8,0},{12,4},{1,9},{5,13},{9,1},{13,5},{2,10},{6,14},... | collective-permute-start | bytes 1597448 | tf_op jit(solution)/shard_map/ppermute | solution.py:98
  416.6 85.6 %collective-permute-start.15 = (bf16[1040,256]{1,0:T(8,128)(2,1)S(1)}, bf16[1040,256]{1,0:T(8,128)(2,1)S(1)}, u32[]{:S(2)}, u32[]{:S(2)}) collective-permute-start(bf16[1040,256]{1,0:T(8,128)(2,1)S(1)} %fusion.367), channel_id=1, source_target_pairs={{0,4},{4,8},{8,12},{12,0},{1,5},{5,9},{9,13},{13,1},{2,6},{6,10},{... | collective-permute-start | bytes 1597448 | tf_op jit(solution)/shard_map/ppermute | solution.py:98
  417.1 85.1 %collective-permute-start.16 = (bf16[1040,256]{1,0:T(8,128)(2,1)S(1)}, bf16[1040,256]{1,0:T(8,128)(2,1)S(1)}, u32[]{:S(2)}, u32[]{:S(2)}) collective-permute-start(bf16[1040,256]{1,0:T(8,128)(2,1)S(1)} %fusion.368), channel_id=1, source_target_pairs={{0,12},{4,0},{8,4},{12,8},{1,13},{5,1},{9,5},{13,9},{2,14},{6,2},{... | collective-permute-start | bytes 1597448 | tf_op jit(solution)/shard_map/ppermute | solution.py:98
  476.5 32.3 %collective-permute-start.19 = (bf16[1040,256]{1,0:T(8,128)(2,1)S(1)}, bf16[1040,256]{1,0:T(8,128)(2,1)S(1)}, u32[]{:S(2)}, u32[]{:S(2)}) collective-permute-start(bf16[1040,256]{1,0:T(8,128)(2,1)S(1)} %fusion.371), channel_id=1, source_target_pairs={{0,12},{4,0},{8,4},{12,8},{1,13},{5,1},{9,5},{13,9},{2,14},{6,2},{... | collective-permute-start | bytes 1597448 | tf_op jit(solution)/shard_map/ppermute | solution.py:98
  510.0 22.5 %collective-permute-start.21 = (bf16[1024,256]{1,0:T(8,128)(2,1)S(1)}, bf16[1024,256]{1,0:T(8,128)(2,1)S(1)}, u32[]{:S(2)}, u32[]{:S(2)}) collective-permute-start(bf16[1024,256]{1,0:T(8,128)(2,1)S(1)} %fusion.294), channel_id=1, source_target_pairs={{0,16},{16,0},{1,17},{17,1},{2,18},{18,2},{3,19},{19,3},{4,20},{20... | collective-permute-start | bytes 1572872 | tf_op jit(solution)/shard_map/ppermute | solution.py:98
  (19 other events, 141.6 us)
Sparse Core Ops, SparseCore 0:
  33.4 46.1 all-gather.8
  81.2 45.3 all-gather.12
  137.9 25.1 all-gather.10
  164.5 23.3 all-gather.14

commit v3 on v2

--- a/solution.py
+++ b/solution.py
@@ -1,6 +1,9 @@
+import functools
 import jax
 import jax.numpy as jnp
 from jax import lax
+from jax.experimental import pallas as pl
+from jax.experimental.pallas import tpu as pltpu
 from jax.sharding import PartitionSpec as P
 
 epsilon = 1e-06
@@ -118,17 +121,82 @@
     return sorted(range(1, n), key=lambda s: -min(s, n - s)) + [0]
 
 
+def split(x):
+    high = x.astype(jnp.bfloat16)
+    return high, (x - high.astype(jnp.float32)).astype(jnp.bfloat16)
+
+
+def product_kernel(coded, index_ref, a_ref, b_ref, out_ref, a_high, a_low):
+    @pl.when(pl.program_id(0) == 0)
+    def _():
+        a_high[...], a_low[...] = split(a_ref[0])
+
+    b_high, b_low = split(b_ref[...])
+    dot = functools.partial(
+        lax.dot_general,
+        dimension_numbers=contract_last,
+        preferred_element_type=jnp.float32,
+    )
+    high, low = a_high[...], a_low[...]
+    term = dot(high, b_high) + (dot(high, b_low) + dot(low, b_high))
+    if not coded:
+        out_ref[...] = term
+        return
+    rows, columns = term.shape
+    tops = []
+    for g in range(rows // GROUP):
+        at = slice(g * GROUP, (g + 1) * GROUP)
+        x = term[at]
+        size = jnp.abs(x)
+        top = jnp.max(size, axis=0, keepdims=True)
+        top = (jnp.maximum(top, 1e-30) * 1.0078125).astype(jnp.bfloat16)
+        top = top.astype(jnp.float32)
+        power = jnp.exp2(size * (SPAN / top) + LOW)
+        out_ref[at, :] = jnp.where(x < 0, -power, power).astype(jnp.bfloat16)
+        tops.append(top)
+    tops.append(jnp.zeros((16 - len(tops), columns), jnp.float32))
+    out_ref[rows:, :] = jnp.concatenate(tops, axis=0).astype(jnp.bfloat16)
+
+
+def product(blocks, index, other, coded):
+    rows, depth = blocks.shape[1:]
+    columns = other.shape[0]
+    tile = min(256, columns)
+    out_rows = rows + 16 if coded else rows
+    return pl.pallas_call(
+        functools.partial(product_kernel, coded),
+        out_shape=jax.ShapeDtypeStruct(
+            (out_rows, columns), jnp.bfloat16 if coded else jnp.float32
+        ),
+        grid_spec=pltpu.PrefetchScalarGridSpec(
+            num_scalar_prefetch=1,
+            grid=(columns // tile,),
+            in_specs=[
+                pl.BlockSpec((1, rows, depth), lambda n, index: (index[0], 0, 0)),
+                pl.BlockSpec((tile, depth), lambda n, index: (n, 0)),
+            ],
+            out_specs=pl.BlockSpec((out_rows, tile), lambda n, index: (0, n)),
+            scratch_shapes=[pltpu.VMEM((rows, depth), jnp.bfloat16)] * 2,
+        ),
+        compiler_params=pltpu.CompilerParams(vmem_limit_bytes=40 * 2**20),
+        cost_estimate=pl.CostEstimate(
+            flops=6 * rows * depth * columns,
+            bytes_accessed=4 * (rows + columns) * depth + 2 * rows * columns,
+            transcendentals=0,
+        ),
+    )(index.astype(jnp.int32).reshape(1), blocks, other)
+
+
 def scatter_products(blocks, other, axis):
     n = lax.axis_size(axis)
     i = lax.axis_index(axis)
     sent, own = [], None
     for step in order_of(n):
-        block = lax.dynamic_index_in_dim(blocks, lax.rem(i + step, n), 0, False)
-        term = matmul(block, other, contract_last)
+        index = lax.rem(i + step, n)
         if step == 0:
-            own = term
+            own = product(blocks, index, other, False)
         else:
-            sent.append(shift(encode(term), axis, step))
+            sent.append(shift(product(blocks, index, other, True), axis, step))
     return own, sent
 
 

time: 549 us -> 438 us (0.80)
  matrix products: 106 us -> 38.7 us
  Pallas kernels: 0 us -> 54.5 us
  local copies, waits for them, and re-layouts: 90.1 us -> 36.7 us
  other arithmetic: 72 us -> 46.6 us
  waiting for transfers between devices: 232 us -> 216 us
    dot_general x22 -> x6, matrix products: 106 us -> 38.7 us  [matmul(): lax.dot_general(a, b, dims, precision=lax.Precision.HIGH, preferred_eleme...]
    pallas_call x0 -> x16, Pallas kernels: none -> 54.5 us  [product(): pl.pallas_call(functools.partial(product_kernel, coded), out_shape=jax.Sh...]
    ppermute x22, waiting for transfers between devices: 209 us -> 193 us  [shift(): return lax.ppermute(x, axis, [(s, (s + step) % n) for s in range(n)])]
    reshape x6 -> x0, local copies, waits for them, and re-layouts: 15.3 us -> none  [encode(): top = jnp.max(jnp.abs(x).reshape(groups, GROUP, columns), axis=1)]
    reduce_max x9 -> x3, other arithmetic: 11.6 us -> 0.5 us  [encode(): top = jnp.max(jnp.abs(x).reshape(groups, GROUP, columns), axis=1)]
    concatenate x6 -> x0, local copies, waits for them, and re-layouts: 10.6 us -> none  [encode(): return jnp.concatenate([code, scale], axis=0)]
    convert_element_type x19 -> x7, other arithmetic: 14.3 us -> 5.1 us  [encode(): code = jnp.where(x < 0, -power, power).astype(jnp.bfloat16)]
    unnamed x47 -> x19, local copies, waits for them, and re-layouts: 12.4 us -> 5.16 us
  transfers between devices with their start and end apart: 26 -> 26, of which waited for: 14 -> 17; matrix products, arithmetic and copies ran while one was open for 33% -> 21% of each run, Pallas kernels for 0% -> 9%
where the time goes in v3:
time: 438 us; the launch traced here: 430 us
  waiting for transfers between devices  216 us (49%)
  Pallas kernels  54.5 us (12%)
  other arithmetic  46.6 us (11%)
  matrix products  38.7 us (9%)
  local copies, waits for them, and re-layouts  36.7 us (8%)
  starting transfers between devices  23.7 us (5%)
  between operations  14.1 us (3%)
    ppermute x22, waiting for transfers between devices, shift(): return lax.ppermute(x, axis, [(s, (s + step) % n) for s in range(n)])  193 us
    pallas_call x16, Pallas kernels, product(): pl.pallas_call(functools.partial(product_kernel, coded), out_shape=jax.Sh...  54.5 us
    dot_general x6, matrix products, matmul(): lax.dot_general(a, b, dims, precision=lax.Precision.HIGH, preferred_eleme...  38.7 us
    ppermute x22, starting transfers between devices, shift(): return lax.ppermute(x, axis, [(s, (s + step) % n) for s in range(n)])  23 us
    all_gather x2, waiting for transfers between devices, pair_body(): gathered = lax.all_gather(part, 'col', axis=0)  22.9 us
    dynamic_update_slice x4, other arithmetic, pair_body(): lax.dynamic_update_slice(left, decode(piece)[None], (place, (1 - me) * ta...  10.7 us
    select_n x19, other arithmetic, decode(): return jnp.where(code < 0, -size, size)  10.5 us
  transfers between devices with their start and end apart: 26, of which 17 were waited for; matrix products, arithmetic and copies ran while one was open for 21% of the time, Pallas kernels for 9%

profile of v3, /device:TPU:16, one launch (start us, length us, event | category | flops | bytes accessed | tf_op | source)
XLA Modules:
  0.0 430.4 jit_solution(170502412641701683)
XLA Ops:
  10.4 12.8 %collective-permute-done.5 = bf16[1024,256]{1,0:T(8,128)(2,1)S(1)} collective-permute-done((bf16[1024,256]{1,0:T(8,128)(2,1)S(1)}, bf16[1024,256]{1,0:T(8,128)(2,1)S(1)}, u32[]{:S(2)}, u32[]{:S(2)}) %collective-permute-start.5) | collective-permute-done | bytes 524320 | tf_op jit(solution)/shard_map/ppermute | solution.py:101
  24.6 8.6 %collective-permute-done.4 = bf16[1024,256]{1,0:T(8,128)(2,1)S(1)} collective-permute-done((bf16[1024,256]{1,0:T(8,128)(2,1)S(1)}, bf16[1024,256]{1,0:T(8,128)(2,1)S(1)}, u32[]{:S(2)}, u32[]{:S(2)}) %collective-permute-start.4) | collective-permute-done | bytes 524320 | tf_op jit(solution)/shard_map/ppermute | solution.py:101
  40.0 7.9 %broadcast_in_dim.108 = f32[4,1024,1024]{2,1,0:T(8,128)} broadcast(f32[]{:T(128)} %constant.150.clone.1), dimensions={} | broadcast | bytes 16777220 | tf_op jit(solution)/shard_map/broadcast_in_dim | solution.py:232
  47.9 8.3 %constant_dynamic-update-slice_fusion.2 = f32[4,1024,1024]{2,1,0:T(8,128)} fusion(f32[4,1024,1024]{2,1,0:T(8,128)} %broadcast_in_dim.108, f32[4,512,1024]{2,1,0:T(8,128)} %param.6, s32[]{:T(128)S(6)} %select_n.221), kind=kLoop, calls=%fused_computation.558 | loop fusion | bytes 16777220 | tf_op jit(solution)/shard_map/dynamic_update_slice | solution.py:233
  56.2 7.0 %collective-permute-done = bf16[528,1024]{1,0:T(8,128)(2,1)S(1)} collective-permute-done((bf16[528,1024]{1,0:T(8,128)(2,1)S(1)}, bf16[528,1024]{1,0:T(8,128)(2,1)S(1)}, u32[]{:S(2)}, u32[]{:S(2)}) %collective-permute-start) | collective-permute-done | bytes 1081376 | tf_op jit(solution)/shard_map/ppermute | solution.py:101
  70.3 18.4 %collective-permute-done.1 = bf16[528,1024]{1,0:T(8,128)(2,1)} collective-permute-done((bf16[528,1024]{1,0:T(8,128)(2,1)S(1)}, bf16[528,1024]{1,0:T(8,128)(2,1)}, u32[]{:S(2)}, u32[]{:S(2)}) %collective-permute-start.1) | collective-permute-done | bytes 1081376 | tf_op jit(solution)/shard_map/ppermute | solution.py:101
  90.1 21.4 %collective-permute-done.3 = bf16[528,1024]{1,0:T(8,128)(2,1)} collective-permute-done((bf16[528,1024]{1,0:T(8,128)(2,1)S(1)}, bf16[528,1024]{1,0:T(8,128)(2,1)}, u32[]{:S(2)}, u32[]{:S(2)}) %collective-permute-start.3) | collective-permute-done | bytes 1081376 | tf_op jit(solution)/shard_map/ppermute | solution.py:101
  125.2 11.2 %bitcast_reduce_fusion.4 = (f32[2,1024]{1,0:T(2,128)S(1)}, f32[256,1024]{1,0:T(8,128)S(1)}) fusion(f32[4096,1024]{1,0:T(8,128)} %bitcast.35, f32[1024,256]{1,0:T(8,128)S(1)} %get-tuple-element.37, f32[1024,256]{1,0:T(8,128)S(1)} %get-tuple-element.38, f32[1024,256]{1,0:T(8,128)S(1)} %get-tuple-element.39, f32[1024,256]{1,0:T(8,128)S(1)} %get-tuple-element.36), kind=kOutput, calls=%fused_computation.325 | convolution fusion | flops 6446118912 | bytes 22028288 | tf_op jit(solution)/shard_map/dot_general | solution.py:68
  141.8 11.2 %bitcast_reduce_fusion.2 = (f32[2,1024]{1,0:T(2,128)S(1)}, f32[256,1024]{1,0:T(8,128)S(1)}) fusion(f32[4096,1024]{1,0:T(8,128)} %bitcast.35, f32[1024,256]{1,0:T(8,128)S(1)} %get-tuple-element.29, f32[1024,256]{1,0:T(8,128)S(1)} %get-tuple-element.30, f32[1024,256]{1,0:T(8,128)S(1)} %get-tuple-element.31, f32[1024,256]{1,0:T(8,128)S(1)} %get-tuple-element.28), kind=kOutput, calls=%fused_computation.315 | convolution fusion | flops 6446118912 | bytes 22028288 | tf_op jit(solution)/shard_map/dot_general | solution.py:68
  154.3 8.5 %fusion.357 = (f32[4,256,1024]{2,1,0:T(8,128)}, f32[4,256,1024]{2,1,0:T(8,128)}) fusion(f32[4,512,1024]{2,1,0:T(8,128)} %a_ref.15), kind=kLoop, calls=%fused_computation.585 | loop fusion | bytes 16777216 | tf_op jit(solution)/shard_map/slice | solution.py:249
  165.1 22.7 %all-gather.15.cloned.1.call-done = bf16[1088,1024]{1,0:T(8,128)(2,1)} async-done(((bf16[272,1024]{1,0:T(8,128)(2,1)}), bf16[1088,1024]{1,0:T(8,128)(2,1)}) %all-gather.15.cloned.1.call-update) | async-done | bytes 2228240 | tf_op jit(solution)/shard_map/all_gather | solution.py:248
  208.0 19.2 %collective-permute-done.6 = bf16[528,1024]{1,0:T(8,128)(2,1)S(1)} collective-permute-done((bf16[528,1024]{1,0:T(8,128)(2,1)S(1)}, bf16[528,1024]{1,0:T(8,128)(2,1)S(1)}, u32[]{:S(2)}, u32[]{:S(2)}) %collective-permute-start.6) | collective-permute-done | bytes 1081376 | tf_op jit(solution)/shard_map/ppermute | solution.py:101
  227.2 4.8 %bitcast_reduce_fusion = (f32[4,1024]{1,0:T(4,128)S(1)}, f32[512,1024]{1,0:T(8,128)S(1)}) fusion(f32[1024]{0:T(1024)S(1)} %copy-done.5, f32[512]{0:T(512)S(1)} %dynamic-slice.34, f32[4,1024]{1,0:T(4,128)S(1)} %convert_multiply_fusion.1, bf16[528,1024]{1,0:T(8,128)(2,1)S(1)} %collective-permute-done.6, f32[512,1024]{1,0:T(8,128)S(1)} %fusion.64, ...), kind=kOutput, calls=%fused_computation.117 | convolution fusion | flops 3230658560 | bytes 11573248 | tf_op jit(solution)/shard_map/dot_general | solution.py:68
  276.0 8.3 %collective-permute-done.11 = bf16[528,512]{1,0:T(8,128)(2,1)S(1)} collective-permute-done((bf16[528,512]{1,0:T(8,128)(2,1)S(1)}, bf16[528,512]{1,0:T(8,128)(2,1)S(1)}, u32[]{:S(2)}, u32[]{:S(2)}) %collective-permute-start.11) | collective-permute-done | bytes 540704 | tf_op jit(solution)/shard_map/ppermute | solution.py:101
  284.3 5.7 %collective-permute-done.13 = bf16[528,512]{1,0:T(8,128)(2,1)S(1)} collective-permute-done((bf16[528,512]{1,0:T(8,128)(2,1)S(1)}, bf16[528,512]{1,0:T(8,128)(2,1)S(1)}, u32[]{:S(2)}, u32[]{:S(2)}) %collective-permute-start.13) | collective-permute-done | bytes 540704 | tf_op jit(solution)/shard_map/ppermute | solution.py:101
  293.8 4.2 shard_map.68
  298.0 4.2 shard_map.69
  302.2 4.2 shard_map.65
  306.4 4.2 shard_map.66
  317.1 4.2 shard_map.67
  333.9 35.5 %collective-permute-done.14 = bf16[1040,256]{1,0:T(8,128)(2,1)S(1)} collective-permute-done((bf16[1040,256]{1,0:T(8,128)(2,1)S(1)}, bf16[1040,256]{1,0:T(8,128)(2,1)S(1)}, u32[]{:S(2)}, u32[]{:S(2)}) %collective-permute-start.14) | collective-permute-done | bytes 532512 | tf_op jit(solution)/shard_map/ppermute | solution.py:101
  369.4 22.8 %collective-permute-done.16 = bf16[1040,256]{1,0:T(8,128)(2,1)S(1)} collective-permute-done((bf16[1040,256]{1,0:T(8,128)(2,1)S(1)}, bf16[1040,256]{1,0:T(8,128)(2,1)S(1)}, u32[]{:S(2)}, u32[]{:S(2)}) %collective-permute-start.16) | collective-permute-done | bytes 532512 | tf_op jit(solution)/shard_map/ppermute | solution.py:101
  393.6 12.8 %collective-permute-done.18 = bf16[1040,256]{1,0:T(8,128)(2,1)S(1)} collective-permute-done((bf16[1040,256]{1,0:T(8,128)(2,1)S(1)}, bf16[1040,256]{1,0:T(8,128)(2,1)S(1)}, u32[]{:S(2)}, u32[]{:S(2)}) %collective-permute-start.18) | collective-permute-done | bytes 532512 | tf_op jit(solution)/shard_map/ppermute | solution.py:101
  408.3 13.3 %collective-permute-done.21 = bf16[1024,256]{1,0:T(8,128)(2,1)S(1)} collective-permute-done((bf16[1024,256]{1,0:T(8,128)(2,1)S(1)}, bf16[1024,256]{1,0:T(8,128)(2,1)S(1)}, u32[]{:S(2)}, u32[]{:S(2)}) %collective-permute-start.21) | collective-permute-done | bytes 524320 | tf_op jit(solution)/shard_map/ppermute | solution.py:101
  (182 shorter events, 134.7 us)
Async XLA Ops:
  6.5 115.1 %all-gather.9.cloned.1.call-start = ((), (), s32[]{:S(2)}) async-start(), calls=%async_computation | async-start | bytes 2662400 | tf_op jit(solution)/shard_map/all_gather | solution.py:245
  8.3 14.9 %collective-permute-start.5 = (bf16[1024,256]{1,0:T(8,128)(2,1)S(1)}, bf16[1024,256]{1,0:T(8,128)(2,1)S(1)}, u32[]{:S(2)}, u32[]{:S(2)}) collective-permute-start(bf16[1024,256]{1,0:T(8,128)(2,1)S(1)} %get-tuple-element.50), channel_id=1, source_target_pairs={{0,16},{16,0},{1,17},{17,1},{2,18},{18,2},{3,19},{19,3},{4,20},{20... | collective-permute-start | bytes 1572872 | tf_op jit(solution)/shard_map/ppermute | solution.py:101
  9.9 23.4 %collective-permute-start.4 = (bf16[1024,256]{1,0:T(8,128)(2,1)S(1)}, bf16[1024,256]{1,0:T(8,128)(2,1)S(1)}, u32[]{:S(2)}, u32[]{:S(2)}) collective-permute-start(bf16[1024,256]{1,0:T(8,128)(2,1)S(1)} %get-tuple-element.51), channel_id=1, source_target_pairs={{0,16},{16,0},{1,17},{17,1},{2,18},{18,2},{3,19},{19,3},{4,20},{20... | collective-permute-start | bytes 1572872 | tf_op jit(solution)/shard_map/ppermute | solution.py:101
  33.3 104.9 %all-gather.13.cloned.1.call-start = ((), (), s32[]{:S(2)}) async-start(), calls=%async_computation.2 | async-start | bytes 2662400 | tf_op jit(solution)/shard_map/all_gather | solution.py:245
  38.4 24.8 %collective-permute-start = (bf16[528,1024]{1,0:T(8,128)(2,1)S(1)}, bf16[528,1024]{1,0:T(8,128)(2,1)S(1)}, u32[]{:S(2)}, u32[]{:S(2)}) collective-permute-start(bf16[528,1024]{1,0:T(8,128)(2,1)S(1)} %fusion.102), channel_id=1, source_target_pairs={{0,16},{16,0},{1,17},{17,1},{2,18},{18,2},{3,19},{19,3},{4,20},{20... | collective-permute-start | bytes 3244040 | tf_op jit(solution)/shard_map/ppermute | solution.py:101
  63.2 25.5 %collective-permute-start.1 = (bf16[528,1024]{1,0:T(8,128)(2,1)S(1)}, bf16[528,1024]{1,0:T(8,128)(2,1)}, u32[]{:S(2)}, u32[]{:S(2)}) collective-permute-start(bf16[528,1024]{1,0:T(8,128)(2,1)S(1)} %collective-permute-done), channel_id=1, source_target_pairs={{0,1},{1,2},{2,3},{3,0},{4,5},{5,6},{6,7},{7,4},{8,9},{9,10},{10,1... | collective-permute-start | bytes 3244040 | tf_op jit(solution)/shard_map/ppermute | solution.py:101
  63.4 26.8 %collective-permute-start.2 = (bf16[528,1024]{1,0:T(8,128)(2,1)S(1)}, bf16[528,1024]{1,0:T(8,128)(2,1)S(1)}, u32[]{:S(2)}, u32[]{:S(2)}) collective-permute-start(bf16[528,1024]{1,0:T(8,128)(2,1)S(1)} %collective-permute-done), channel_id=1, source_target_pairs={{0,2},{1,3},{2,0},{3,1},{4,6},{5,7},{6,4},{7,5},{8,10},{9,11},{10,... | collective-permute-start | bytes 3244040 | tf_op jit(solution)/shard_map/ppermute | solution.py:101
  65.4 46.2 %collective-permute-start.3 = (bf16[528,1024]{1,0:T(8,128)(2,1)S(1)}, bf16[528,1024]{1,0:T(8,128)(2,1)}, u32[]{:S(2)}, u32[]{:S(2)}) collective-permute-start(bf16[528,1024]{1,0:T(8,128)(2,1)S(1)} %collective-permute-done), channel_id=1, source_target_pairs={{0,3},{1,0},{2,1},{3,2},{4,7},{5,4},{6,5},{7,6},{8,11},{9,8},{10,9... | collective-permute-start | bytes 3244040 | tf_op jit(solution)/shard_map/ppermute | solution.py:101
  67.7 95.3 %all-gather.11.cloned.1.call-start = ((), (), s32[]{:S(2)}) async-start(), calls=%async_computation.1 | async-start | bytes 2785280 | tf_op jit(solution)/shard_map/all_gather | solution.py:248
  137.7 50.1 %all-gather.15.cloned.1.call-start = ((), (), s32[]{:S(2)}) async-start(), calls=%async_computation.3 | async-start | bytes 2785280 | tf_op jit(solution)/shard_map/all_gather | solution.py:248
  200.9 26.2 %collective-permute-start.6 = (bf16[528,1024]{1,0:T(8,128)(2,1)S(1)}, bf16[528,1024]{1,0:T(8,128)(2,1)S(1)}, u32[]{:S(2)}, u32[]{:S(2)}) collective-permute-start(bf16[528,1024]{1,0:T(8,128)(2,1)S(1)} %fusion.103), channel_id=1, source_target_pairs={{0,16},{16,0},{1,17},{17,1},{2,18},{18,2},{3,19},{19,3},{4,20},{20... | collective-permute-start | bytes 3244040 | tf_op jit(solution)/shard_map/ppermute | solution.py:101
  233.7 25.5 %collective-permute-start.10 = (bf16[528,1024]{1,0:T(8,128)(2,1)}, bf16[528,1024]{1,0:T(8,128)(2,1)}, u32[]{:S(2)}, u32[]{:S(2)}) collective-permute-start(bf16[528,1024]{1,0:T(8,128)(2,1)} %fusion.104), channel_id=1, source_target_pairs={{0,16},{16,0},{1,17},{17,1},{2,18},{18,2},{3,19},{19,3},{4,20},{20... | collective-permute-start | bytes 3244040 | tf_op jit(solution)/shard_map/ppermute | solution.py:101
  240.7 15.4 %collective-permute-start.7 = (bf16[528,512]{1,0:T(8,128)(2,1)S(1)}, bf16[528,512]{1,0:T(8,128)(2,1)}, u32[]{:S(2)}, u32[]{:S(2)}) collective-permute-start(bf16[528,512]{1,0:T(8,128)(2,1)S(1)} %shard_map.56), channel_id=1, source_target_pairs={{0,2},{1,3},{2,0},{3,1},{4,6},{5,7},{6,4},{7,5},{8,10},{9,11},{10,... | collective-permute-start | bytes 1622024 | tf_op jit(solution)/shard_map/ppermute | solution.py:101
  247.4 22.3 %collective-permute-start.9 = (bf16[528,512]{1,0:T(8,128)(2,1)S(1)}, bf16[528,512]{1,0:T(8,128)(2,1)S(1)}, u32[]{:S(2)}, u32[]{:S(2)}) collective-permute-start(bf16[528,512]{1,0:T(8,128)(2,1)S(1)} %shard_map.58), channel_id=1, source_target_pairs={{0,3},{1,0},{2,1},{3,2},{4,7},{5,4},{6,5},{7,6},{8,11},{9,8},{10,9... | collective-permute-start | bytes 1622024 | tf_op jit(solution)/shard_map/ppermute | solution.py:101
  269.0 15.3 %collective-permute-start.11 = (bf16[528,512]{1,0:T(8,128)(2,1)S(1)}, bf16[528,512]{1,0:T(8,128)(2,1)S(1)}, u32[]{:S(2)}, u32[]{:S(2)}) collective-permute-start(bf16[528,512]{1,0:T(8,128)(2,1)S(1)} %shard_map.60), channel_id=1, source_target_pairs={{0,2},{1,3},{2,0},{3,1},{4,6},{5,7},{6,4},{7,5},{8,10},{9,11},{10,... | collective-permute-start | bytes 1622024 | tf_op jit(solution)/shard_map/ppermute | solution.py:101
  272.3 17.7 %collective-permute-start.13 = (bf16[528,512]{1,0:T(8,128)(2,1)S(1)}, bf16[528,512]{1,0:T(8,128)(2,1)S(1)}, u32[]{:S(2)}, u32[]{:S(2)}) collective-permute-start(bf16[528,512]{1,0:T(8,128)(2,1)S(1)} %shard_map.62), channel_id=1, source_target_pairs={{0,3},{1,0},{2,1},{3,2},{4,7},{5,4},{6,5},{7,6},{8,11},{9,8},{10,9... | collective-permute-start | bytes 1622024 | tf_op jit(solution)/shard_map/ppermute | solution.py:101
  310.6 58.8 %collective-permute-start.14 = (bf16[1040,256]{1,0:T(8,128)(2,1)S(1)}, bf16[1040,256]{1,0:T(8,128)(2,1)S(1)}, u32[]{:S(2)}, u32[]{:S(2)}) collective-permute-start(bf16[1040,256]{1,0:T(8,128)(2,1)S(1)} %shard_map.65), channel_id=1, source_target_pairs={{0,8},{4,12},{8,0},{12,4},{1,9},{5,13},{9,1},{13,5},{2,10},{6,14},... | collective-permute-start | bytes 1597448 | tf_op jit(solution)/shard_map/ppermute | solution.py:101
  311.2 58.2 %collective-permute-start.15 = (bf16[1040,256]{1,0:T(8,128)(2,1)S(1)}, bf16[1040,256]{1,0:T(8,128)(2,1)S(1)}, u32[]{:S(2)}, u32[]{:S(2)}) collective-permute-start(bf16[1040,256]{1,0:T(8,128)(2,1)S(1)} %shard_map.66), channel_id=1, source_target_pairs={{0,4},{4,8},{8,12},{12,0},{1,5},{5,9},{9,13},{13,1},{2,6},{6,10},{... | collective-permute-start | bytes 1597448 | tf_op jit(solution)/shard_map/ppermute | solution.py:101
  321.3 72.2 %collective-permute-start.17 = (bf16[1040,256]{1,0:T(8,128)(2,1)S(1)}, bf16[1040,256]{1,0:T(8,128)(2,1)S(1)}, u32[]{:S(2)}, u32[]{:S(2)}) collective-permute-start(bf16[1040,256]{1,0:T(8,128)(2,1)S(1)} %shard_map.68), channel_id=1, source_target_pairs={{0,8},{4,12},{8,0},{12,4},{1,9},{5,13},{9,1},{13,5},{2,10},{6,14},... | collective-permute-start | bytes 1597448 | tf_op jit(solution)/shard_map/ppermute | solution.py:101
  323.8 82.6 %collective-permute-start.18 = (bf16[1040,256]{1,0:T(8,128)(2,1)S(1)}, bf16[1040,256]{1,0:T(8,128)(2,1)S(1)}, u32[]{:S(2)}, u32[]{:S(2)}) collective-permute-start(bf16[1040,256]{1,0:T(8,128)(2,1)S(1)} %shard_map.69), channel_id=1, source_target_pairs={{0,4},{4,8},{8,12},{12,0},{1,5},{5,9},{9,13},{13,1},{2,6},{6,10},{... | collective-permute-start | bytes 1597448 | tf_op jit(solution)/shard_map/ppermute | solution.py:101
  323.8 68.4 %collective-permute-start.16 = (bf16[1040,256]{1,0:T(8,128)(2,1)S(1)}, bf16[1040,256]{1,0:T(8,128)(2,1)S(1)}, u32[]{:S(2)}, u32[]{:S(2)}) collective-permute-start(bf16[1040,256]{1,0:T(8,128)(2,1)S(1)} %shard_map.67), channel_id=1, source_target_pairs={{0,12},{4,0},{8,4},{12,8},{1,13},{5,1},{9,5},{13,9},{2,14},{6,2},{... | collective-permute-start | bytes 1597448 | tf_op jit(solution)/shard_map/ppermute | solution.py:101
  369.4 37.0 %collective-permute-start.19 = (bf16[1040,256]{1,0:T(8,128)(2,1)S(1)}, bf16[1040,256]{1,0:T(8,128)(2,1)S(1)}, u32[]{:S(2)}, u32[]{:S(2)}) collective-permute-start(bf16[1040,256]{1,0:T(8,128)(2,1)S(1)} %shard_map.70), channel_id=1, source_target_pairs={{0,12},{4,0},{8,4},{12,8},{1,13},{5,1},{9,5},{13,9},{2,14},{6,2},{... | collective-permute-start | bytes 1597448 | tf_op jit(solution)/shard_map/ppermute | solution.py:101
  393.5 14.8 %collective-permute-start.20 = (bf16[1024,256]{1,0:T(8,128)(2,1)S(1)}, bf16[1024,256]{1,0:T(8,128)(2,1)S(1)}, u32[]{:S(2)}, u32[]{:S(2)}) collective-permute-start(bf16[1024,256]{1,0:T(8,128)(2,1)S(1)} %fusion.208), channel_id=1, source_target_pairs={{0,16},{16,0},{1,17},{17,1},{2,18},{18,2},{3,19},{19,3},{4,20},{20... | collective-permute-start | bytes 1572872 | tf_op jit(solution)/shard_map/ppermute | solution.py:101
  407.6 14.0 %collective-permute-start.21 = (bf16[1024,256]{1,0:T(8,128)(2,1)S(1)}, bf16[1024,256]{1,0:T(8,128)(2,1)S(1)}, u32[]{:S(2)}, u32[]{:S(2)}) collective-permute-start(bf16[1024,256]{1,0:T(8,128)(2,1)S(1)} %fusion.212), channel_id=1, source_target_pairs={{0,16},{16,0},{1,17},{17,1},{2,18},{18,2},{3,19},{19,3},{4,20},{20... | collective-permute-start | bytes 1572872 | tf_op jit(solution)/shard_map/ppermute | solution.py:101
  (11 other events, 113.7 us)
Sparse Core Ops, SparseCore 0:
  33.4 46.1 all-gather.8
  81.2 45.3 all-gather.12
  137.8 25.1 all-gather.10
  164.5 23.3 all-gather.14

commit v4 on v3

--- a/solution.py
+++ b/solution.py
@@ -245,8 +245,18 @@
         stacked = lax.all_gather(coded[c], "row", axis=0)
         stacked = jnp.concatenate([decode(s) for s in stacked], axis=0)
         part = encode(matmul(stacked, left_flat, contract_first))
-        gathered = lax.all_gather(part, "col", axis=0)
-        r = right_basis[:, c * w : (c + 1) * w].reshape(-1, columns)
+        gathered = [part] + [shift(part, "col", step) for step in range(1, cols)]
+        r = jnp.concatenate(
+            [
+                lax.dynamic_slice(
+                    right_basis,
+                    (lax.rem(col - step + cols, cols), c * w, 0),
+                    (1, w, columns),
+                )[0]
+                for step in range(cols)
+            ],
+            axis=0,
+        )
         for_peer = [decode(half(s, 1 - me, 1)) for s in gathered]
         give = give + matmul(jnp.concatenate(for_peer, axis=0), r, contract_first)
         for_me = [decode(half(s, me, 1)) for s in gathered]

time: 438 us -> 433 us (0.989)
  the two profiles are of different devices: /device:TPU:16 before, /device:TPU:0 now
where the time goes in v4:
time: 433 us; the launch traced here: 427 us
  waiting for transfers between devices  207 us (48%)
  other arithmetic  56.8 us (13%)
  Pallas kernels  53.9 us (12%)
  matrix products  38.4 us (9%)
  starting transfers between devices  31.4 us (7%)
  local copies, waits for them, and re-layouts  25.3 us (6%)
  between operations  14.3 us (3%)
    ppermute x28, waiting for transfers between devices, shift(): return lax.ppermute(x, axis, [(s, (s + step) % n) for s in range(n)])  207 us
    pallas_call x16, Pallas kernels, product(): pl.pallas_call(functools.partial(product_kernel, coded), out_shape=jax.Sh...  53.9 us
    dot_general x6, matrix products, matmul(): lax.dot_general(a, b, dims, precision=lax.Precision.HIGH, preferred_eleme...  38.4 us
    ppermute x28, starting transfers between devices, shift(): return lax.ppermute(x, axis, [(s, (s + step) % n) for s in range(n)])  31.4 us
    select_n x11, other arithmetic, decode(): return jnp.where(code < 0, -size, size)  14.7 us
    dynamic_update_slice x4, other arithmetic, pair_body(): lax.dynamic_update_slice(left, decode(piece)[None], (place, (1 - me) * ta...  13.2 us
    mul x28, other arithmetic, decode(): top = coded[rows:rows + groups].astype(jnp.float32) * (1.0 / SPAN)  9.47 us
  transfers between devices with their start and end apart: 30, of which 18 were waited for; matrix products, arithmetic and copies ran while one was open for 22% of the time, Pallas kernels for 9%

profile of v4, /device:TPU:0, one launch (start us, length us, event | category | flops | bytes accessed | tf_op | source)
XLA Modules:
  0.0 427.3 jit_solution(1972377420834053683)
XLA Ops:
  11.4 12.7 %collective-permute-done.5 = bf16[1024,256]{1,0:T(8,128)(2,1)S(1)} collective-permute-done((bf16[1024,256]{1,0:T(8,128)(2,1)S(1)}, bf16[1024,256]{1,0:T(8,128)(2,1)S(1)}, u32[]{:S(2)}, u32[]{:S(2)}) %collective-permute-start.5) | collective-permute-done | bytes 524320 | tf_op jit(solution)/shard_map/ppermute | solution.py:101
  25.5 8.9 %collective-permute-done.4 = bf16[1024,256]{1,0:T(8,128)(2,1)S(1)} collective-permute-done((bf16[1024,256]{1,0:T(8,128)(2,1)S(1)}, bf16[1024,256]{1,0:T(8,128)(2,1)S(1)}, u32[]{:S(2)}, u32[]{:S(2)}) %collective-permute-start.4) | collective-permute-done | bytes 524320 | tf_op jit(solution)/shard_map/ppermute | solution.py:101
  42.2 23.4 %collective-permute-done = bf16[528,1024]{1,0:T(8,128)(2,1)} collective-permute-done((bf16[528,1024]{1,0:T(8,128)(2,1)S(1)}, bf16[528,1024]{1,0:T(8,128)(2,1)}, u32[]{:S(2)}, u32[]{:S(2)}) %collective-permute-start) | collective-permute-done | bytes 1081376 | tf_op jit(solution)/shard_map/ppermute | solution.py:101
  65.6 7.9 %broadcast_in_dim.108 = f32[4,1024,1024]{2,1,0:T(8,128)} broadcast(f32[]{:T(128)} %constant.135.clone.1), dimensions={} | broadcast | bytes 16777220 | tf_op jit(solution)/shard_map/broadcast_in_dim | solution.py:232
  73.5 8.4 %constant_dynamic-update-slice_fusion = f32[4,1024,1024]{2,1,0:T(8,128)} fusion(f32[4,1024,1024]{2,1,0:T(8,128)} %broadcast_in_dim.108, f32[4,512,1024]{2,1,0:T(8,128)} %param.6, s32[]{:T(128)S(6)} %select_n.229), kind=kLoop, calls=%fused_computation.514 | loop fusion | bytes 16777220 | tf_op jit(solution)/shard_map/dynamic_update_slice | solution.py:233
  92.5 16.0 %collective-permute-done.2 = bf16[528,1024]{1,0:T(8,128)(2,1)} collective-permute-done((bf16[528,1024]{1,0:T(8,128)(2,1)}, bf16[528,1024]{1,0:T(8,128)(2,1)}, u32[]{:S(2)}, u32[]{:S(2)}) %collective-permute-start.2) | collective-permute-done | bytes 1081376 | tf_op jit(solution)/shard_map/ppermute | solution.py:101
  109.2 10.0 %collective-permute-done.3 = bf16[528,1024]{1,0:T(8,128)(2,1)} collective-permute-done((bf16[528,1024]{1,0:T(8,128)(2,1)}, bf16[528,1024]{1,0:T(8,128)(2,1)}, u32[]{:S(2)}, u32[]{:S(2)}) %collective-permute-start.3) | collective-permute-done | bytes 1081376 | tf_op jit(solution)/shard_map/ppermute | solution.py:101
  134.3 11.2 %bitcast_reduce_fusion.2 = (f32[2,1024]{1,0:T(2,128)S(1)}, f32[256,1024]{1,0:T(8,128)S(1)}) fusion(f32[4096,1024]{1,0:T(8,128)} %bitcast.324, f32[1024,256]{1,0:T(8,128)S(1)} %get-tuple-element.33, f32[1024,256]{1,0:T(8,128)S(1)} %get-tuple-element.34, f32[1024,256]{1,0:T(8,128)S(1)} %get-tuple-element.35, f32[1024,256]{1,0:T(8,128)S(1)} %get-tuple-element.32), kind=kOutput, calls=%fused_computation.316 | convolution fusion | flops 6446118912 | bytes 22028288 | tf_op jit(solution)/shard_map/dot_general | solution.py:68
  153.6 11.2 %bitcast_reduce_fusion.4 = (f32[2,1024]{1,0:T(2,128)S(1)}, f32[256,1024]{1,0:T(8,128)S(1)}) fusion(f32[4096,1024]{1,0:T(8,128)} %bitcast.325, f32[1024,256]{1,0:T(8,128)S(1)} %get-tuple-element.25, f32[1024,256]{1,0:T(8,128)S(1)} %get-tuple-element.26, f32[1024,256]{1,0:T(8,128)S(1)} %get-tuple-element.27, f32[1024,256]{1,0:T(8,128)S(1)} %get-tuple-element.24), kind=kOutput, calls=%fused_computation.326 | convolution fusion | flops 6446118912 | bytes 22028288 | tf_op jit(solution)/shard_map/dot_general | solution.py:68
  179.6 6.4 %collective-permute-done.8 = bf16[272,1024]{1,0:T(8,128)(2,1)S(1)} collective-permute-done((bf16[272,1024]{1,0:T(8,128)(2,1)S(1)}, bf16[272,1024]{1,0:T(8,128)(2,1)S(1)}, u32[]{:S(2)}, u32[]{:S(2)}) %collective-permute-start.8) | collective-permute-done | bytes 557088 | tf_op jit(solution)/shard_map/ppermute | solution.py:101
  186.0 12.7 %collective-permute-done.7 = bf16[272,1024]{1,0:T(8,128)(2,1)S(1)} collective-permute-done((bf16[272,1024]{1,0:T(8,128)(2,1)S(1)}, bf16[272,1024]{1,0:T(8,128)(2,1)S(1)}, u32[]{:S(2)}, u32[]{:S(2)}) %collective-permute-start.7) | collective-permute-done | bytes 557088 | tf_op jit(solution)/shard_map/ppermute | solution.py:101
  213.6 15.2 %collective-permute-done.12 = bf16[528,1024]{1,0:T(8,128)(2,1)S(1)} collective-permute-done((bf16[528,1024]{1,0:T(8,128)(2,1)S(1)}, bf16[528,1024]{1,0:T(8,128)(2,1)S(1)}, u32[]{:S(2)}, u32[]{:S(2)}) %collective-permute-start.12) | collective-permute-done | bytes 1081376 | tf_op jit(solution)/shard_map/ppermute | solution.py:101
  228.8 4.7 %bitcast_reduce_fusion = (f32[4,1024]{1,0:T(4,128)S(1)}, f32[512,1024]{1,0:T(8,128)S(1)}) fusion(f32[1024]{0:T(1024)S(1)} %copy-done.10, f32[512]{0:T(512)S(1)} %dynamic-slice.34, f32[4,1024]{1,0:T(4,128)S(1)} %convert_multiply_fusion.1, bf16[528,1024]{1,0:T(8,128)(2,1)S(1)} %collective-permute-done.12, f32[512,1024]{1,0:T(8,128)S(1)} %fusion.17, ...), kind=kOutput, calls=%fused_computation.119 | convolution fusion | flops 3233804288 | bytes 11573248 | tf_op jit(solution)/shard_map/dot_general | solution.py:68
  272.9 5.3 %collective-permute-done.18 = bf16[528,512]{1,0:T(8,128)(2,1)S(1)} collective-permute-done((bf16[528,512]{1,0:T(8,128)(2,1)S(1)}, bf16[528,512]{1,0:T(8,128)(2,1)S(1)}, u32[]{:S(2)}, u32[]{:S(2)}) %collective-permute-start.18) | collective-permute-done | bytes 540704 | tf_op jit(solution)/shard_map/ppermute | solution.py:101
  278.3 7.9 %collective-permute-done.17 = bf16[528,512]{1,0:T(8,128)(2,1)S(1)} collective-permute-done((bf16[528,512]{1,0:T(8,128)(2,1)S(1)}, bf16[528,512]{1,0:T(8,128)(2,1)S(1)}, u32[]{:S(2)}, u32[]{:S(2)}) %collective-permute-start.17) | collective-permute-done | bytes 540704 | tf_op jit(solution)/shard_map/ppermute | solution.py:101
  289.9 4.2 shard_map.67
  294.1 4.2 shard_map.66
  298.3 4.2 shard_map.70
  314.7 4.2 shard_map.65
  327.4 4.2 shard_map.68
  334.9 22.5 %collective-permute-done.20 = bf16[1040,256]{1,0:T(8,128)(2,1)S(1)} collective-permute-done((bf16[1040,256]{1,0:T(8,128)(2,1)S(1)}, bf16[1040,256]{1,0:T(8,128)(2,1)S(1)}, u32[]{:S(2)}, u32[]{:S(2)}) %collective-permute-start.20) | collective-permute-done | bytes 532512 | tf_op jit(solution)/shard_map/ppermute | solution.py:101
  358.7 10.4 %collective-permute-done.24 = bf16[1040,256]{1,0:T(8,128)(2,1)S(1)} collective-permute-done((bf16[1040,256]{1,0:T(8,128)(2,1)S(1)}, bf16[1040,256]{1,0:T(8,128)(2,1)S(1)}, u32[]{:S(2)}, u32[]{:S(2)}) %collective-permute-start.24) | collective-permute-done | bytes 532512 | tf_op jit(solution)/shard_map/ppermute | solution.py:101
  369.1 34.0 %collective-permute-done.23 = bf16[1040,256]{1,0:T(8,128)(2,1)S(1)} collective-permute-done((bf16[1040,256]{1,0:T(8,128)(2,1)S(1)}, bf16[1040,256]{1,0:T(8,128)(2,1)S(1)}, u32[]{:S(2)}, u32[]{:S(2)}) %collective-permute-start.23) | collective-permute-done | bytes 532512 | tf_op jit(solution)/shard_map/ppermute | solution.py:101
  404.4 13.9 %collective-permute-done.27 = bf16[1024,256]{1,0:T(8,128)(2,1)S(1)} collective-permute-done((bf16[1024,256]{1,0:T(8,128)(2,1)S(1)}, bf16[1024,256]{1,0:T(8,128)(2,1)S(1)}, u32[]{:S(2)}, u32[]{:S(2)}) %collective-permute-start.27) | collective-permute-done | bytes 524320 | tf_op jit(solution)/shard_map/ppermute | solution.py:101
  (186 shorter events, 149.1 us)
Async XLA Ops:
  6.5 124.1 %all-gather.7.cloned.1.call-start = ((), (), s32[]{:S(2)}) async-start(), calls=%async_computation.1 | async-start | bytes 2662400 | tf_op jit(solution)/shard_map/all_gather | solution.py:245
  8.3 15.8 %collective-permute-start.5 = (bf16[1024,256]{1,0:T(8,128)(2,1)S(1)}, bf16[1024,256]{1,0:T(8,128)(2,1)S(1)}, u32[]{:S(2)}, u32[]{:S(2)}) collective-permute-start(bf16[1024,256]{1,0:T(8,128)(2,1)S(1)} %get-tuple-element.46), channel_id=1, source_target_pairs={{0,16},{16,0},{1,17},{17,1},{2,18},{18,2},{3,19},{19,3},{4,20},{20... | collective-permute-start | bytes 1572872 | tf_op jit(solution)/shard_map/ppermute | solution.py:101
  11.3 23.2 %collective-permute-start.4 = (bf16[1024,256]{1,0:T(8,128)(2,1)S(1)}, bf16[1024,256]{1,0:T(8,128)(2,1)S(1)}, u32[]{:S(2)}, u32[]{:S(2)}) collective-permute-start(bf16[1024,256]{1,0:T(8,128)(2,1)S(1)} %get-tuple-element.47), channel_id=1, source_target_pairs={{0,16},{16,0},{1,17},{17,1},{2,18},{18,2},{3,19},{19,3},{4,20},{20... | collective-permute-start | bytes 1572872 | tf_op jit(solution)/shard_map/ppermute | solution.py:101
  36.0 114.0 %all-gather.5.cloned.1.call-start = ((), (), s32[]{:S(2)}) async-start(), calls=%async_computation | async-start | bytes 2662400 | tf_op jit(solution)/shard_map/all_gather | solution.py:245
  40.4 25.2 %collective-permute-start = (bf16[528,1024]{1,0:T(8,128)(2,1)S(1)}, bf16[528,1024]{1,0:T(8,128)(2,1)}, u32[]{:S(2)}, u32[]{:S(2)}) collective-permute-start(bf16[528,1024]{1,0:T(8,128)(2,1)S(1)} %fusion.99), channel_id=1, source_target_pairs={{0,16},{16,0},{1,17},{17,1},{2,18},{18,2},{3,19},{19,3},{4,20},{20... | collective-permute-start | bytes 3244040 | tf_op jit(solution)/shard_map/ppermute | solution.py:101
  65.6 26.2 %collective-permute-start.1 = (bf16[528,1024]{1,0:T(8,128)(2,1)}, bf16[528,1024]{1,0:T(8,128)(2,1)}, u32[]{:S(2)}, u32[]{:S(2)}) collective-permute-start(bf16[528,1024]{1,0:T(8,128)(2,1)} %collective-permute-done), channel_id=1, source_target_pairs={{0,1},{1,2},{2,3},{3,0},{4,5},{5,6},{6,7},{7,4},{8,9},{9,10},{10,1... | collective-permute-start | bytes 3244040 | tf_op jit(solution)/shard_map/ppermute | solution.py:101
  81.9 26.6 %collective-permute-start.2 = (bf16[528,1024]{1,0:T(8,128)(2,1)}, bf16[528,1024]{1,0:T(8,128)(2,1)}, u32[]{:S(2)}, u32[]{:S(2)}) collective-permute-start(bf16[528,1024]{1,0:T(8,128)(2,1)} %collective-permute-done), channel_id=1, source_target_pairs={{0,2},{1,3},{2,0},{3,1},{4,6},{5,7},{6,4},{7,5},{8,10},{9,11},{10,... | collective-permute-start | bytes 3244040 | tf_op jit(solution)/shard_map/ppermute | solution.py:101
  83.3 35.9 %collective-permute-start.3 = (bf16[528,1024]{1,0:T(8,128)(2,1)}, bf16[528,1024]{1,0:T(8,128)(2,1)}, u32[]{:S(2)}, u32[]{:S(2)}) collective-permute-start(bf16[528,1024]{1,0:T(8,128)(2,1)} %collective-permute-done), channel_id=1, source_target_pairs={{0,3},{1,0},{2,1},{3,2},{4,7},{5,4},{6,5},{7,6},{8,11},{9,8},{10,9... | collective-permute-start | bytes 3244040 | tf_op jit(solution)/shard_map/ppermute | solution.py:101
  146.8 23.9 %collective-permute-start.11 = (bf16[272,1024]{1,0:T(8,128)(2,1)}, bf16[272,1024]{1,0:T(8,128)(2,1)}, u32[]{:S(2)}, u32[]{:S(2)}) collective-permute-start(bf16[272,1024]{1,0:T(8,128)(2,1)} %fusion.239), channel_id=1, source_target_pairs={{0,3},{1,0},{2,1},{3,2},{4,7},{5,4},{6,5},{7,6},{8,11},{9,8},{10,9... | collective-permute-start | bytes 1671176 | tf_op jit(solution)/shard_map/ppermute | solution.py:101
  149.0 26.4 %collective-permute-start.10 = (bf16[272,1024]{1,0:T(8,128)(2,1)}, bf16[272,1024]{1,0:T(8,128)(2,1)}, u32[]{:S(2)}, u32[]{:S(2)}) collective-permute-start(bf16[272,1024]{1,0:T(8,128)(2,1)} %fusion.239), channel_id=1, source_target_pairs={{0,2},{1,3},{2,0},{3,1},{4,6},{5,7},{6,4},{7,5},{8,10},{9,11},{10,... | collective-permute-start | bytes 1671176 | tf_op jit(solution)/shard_map/ppermute | solution.py:101
  149.7 27.8 %collective-permute-start.9 = (bf16[272,1024]{1,0:T(8,128)(2,1)}, bf16[272,1024]{1,0:T(8,128)(2,1)}, u32[]{:S(2)}, u32[]{:S(2)}) collective-permute-start(bf16[272,1024]{1,0:T(8,128)(2,1)} %fusion.239), channel_id=1, source_target_pairs={{0,1},{1,2},{2,3},{3,0},{4,5},{5,6},{6,7},{7,4},{8,9},{9,10},{10,1... | collective-permute-start | bytes 1671176 | tf_op jit(solution)/shard_map/ppermute | solution.py:101
  165.2 20.8 %collective-permute-start.8 = (bf16[272,1024]{1,0:T(8,128)(2,1)S(1)}, bf16[272,1024]{1,0:T(8,128)(2,1)S(1)}, u32[]{:S(2)}, u32[]{:S(2)}) collective-permute-start(bf16[272,1024]{1,0:T(8,128)(2,1)S(1)} %fusion.238), channel_id=1, source_target_pairs={{0,3},{1,0},{2,1},{3,2},{4,7},{5,4},{6,5},{7,6},{8,11},{9,8},{10,9... | collective-permute-start | bytes 1671176 | tf_op jit(solution)/shard_map/ppermute | solution.py:101
  167.0 31.7 %collective-permute-start.7 = (bf16[272,1024]{1,0:T(8,128)(2,1)S(1)}, bf16[272,1024]{1,0:T(8,128)(2,1)S(1)}, u32[]{:S(2)}, u32[]{:S(2)}) collective-permute-start(bf16[272,1024]{1,0:T(8,128)(2,1)S(1)} %fusion.238), channel_id=1, source_target_pairs={{0,2},{1,3},{2,0},{3,1},{4,6},{5,7},{6,4},{7,5},{8,10},{9,11},{10,... | collective-permute-start | bytes 1671176 | tf_op jit(solution)/shard_map/ppermute | solution.py:101
  170.7 31.7 %collective-permute-start.6 = (bf16[272,1024]{1,0:T(8,128)(2,1)S(1)}, bf16[272,1024]{1,0:T(8,128)(2,1)S(1)}, u32[]{:S(2)}, u32[]{:S(2)}) collective-permute-start(bf16[272,1024]{1,0:T(8,128)(2,1)S(1)} %fusion.238), channel_id=1, source_target_pairs={{0,1},{1,2},{2,3},{3,0},{4,5},{5,6},{6,7},{7,4},{8,9},{9,10},{10,1... | collective-permute-start | bytes 1671176 | tf_op jit(solution)/shard_map/ppermute | solution.py:101
  208.3 20.5 %collective-permute-start.12 = (bf16[528,1024]{1,0:T(8,128)(2,1)S(1)}, bf16[528,1024]{1,0:T(8,128)(2,1)S(1)}, u32[]{:S(2)}, u32[]{:S(2)}) collective-permute-start(bf16[528,1024]{1,0:T(8,128)(2,1)S(1)} %fusion.100), channel_id=1, source_target_pairs={{0,16},{16,0},{1,17},{17,1},{2,18},{18,2},{3,19},{19,3},{4,20},{20... | collective-permute-start | bytes 3244040 | tf_op jit(solution)/shard_map/ppermute | solution.py:101
  235.3 19.9 %collective-permute-start.16 = (bf16[528,1024]{1,0:T(8,128)(2,1)}, bf16[528,1024]{1,0:T(8,128)(2,1)}, u32[]{:S(2)}, u32[]{:S(2)}) collective-permute-start(bf16[528,1024]{1,0:T(8,128)(2,1)} %fusion.101), channel_id=1, source_target_pairs={{0,16},{16,0},{1,17},{17,1},{2,18},{18,2},{3,19},{19,3},{4,20},{20... | collective-permute-start | bytes 3244040 | tf_op jit(solution)/shard_map/ppermute | solution.py:101
  266.7 19.4 %collective-permute-start.17 = (bf16[528,512]{1,0:T(8,128)(2,1)S(1)}, bf16[528,512]{1,0:T(8,128)(2,1)S(1)}, u32[]{:S(2)}, u32[]{:S(2)}) collective-permute-start(bf16[528,512]{1,0:T(8,128)(2,1)S(1)} %shard_map.60), channel_id=1, source_target_pairs={{0,2},{1,3},{2,0},{3,1},{4,6},{5,7},{6,4},{7,5},{8,10},{9,11},{10,... | collective-permute-start | bytes 1622024 | tf_op jit(solution)/shard_map/ppermute | solution.py:101
  306.8 24.8 %collective-permute-start.22 = (bf16[1040,256]{1,0:T(8,128)(2,1)S(1)}, bf16[1040,256]{1,0:T(8,128)(2,1)S(1)}, u32[]{:S(2)}, u32[]{:S(2)}) collective-permute-start(bf16[1040,256]{1,0:T(8,128)(2,1)S(1)} %shard_map.67), channel_id=1, source_target_pairs={{0,12},{4,0},{8,4},{12,8},{1,13},{5,1},{9,5},{13,9},{2,14},{6,2},{... | collective-permute-start | bytes 1597448 | tf_op jit(solution)/shard_map/ppermute | solution.py:101
  310.5 24.4 %collective-permute-start.21 = (bf16[1040,256]{1,0:T(8,128)(2,1)S(1)}, bf16[1040,256]{1,0:T(8,128)(2,1)S(1)}, u32[]{:S(2)}, u32[]{:S(2)}) collective-permute-start(bf16[1040,256]{1,0:T(8,128)(2,1)S(1)} %shard_map.66), channel_id=1, source_target_pairs={{0,4},{4,8},{8,12},{12,0},{1,5},{5,9},{9,13},{13,1},{2,6},{6,10},{... | collective-permute-start | bytes 1597448 | tf_op jit(solution)/shard_map/ppermute | solution.py:101
  318.9 38.5 %collective-permute-start.20 = (bf16[1040,256]{1,0:T(8,128)(2,1)S(1)}, bf16[1040,256]{1,0:T(8,128)(2,1)S(1)}, u32[]{:S(2)}, u32[]{:S(2)}) collective-permute-start(bf16[1040,256]{1,0:T(8,128)(2,1)S(1)} %shard_map.65), channel_id=1, source_target_pairs={{0,8},{4,12},{8,0},{12,4},{1,9},{5,13},{9,1},{13,5},{2,10},{6,14},... | collective-permute-start | bytes 1597448 | tf_op jit(solution)/shard_map/ppermute | solution.py:101
  320.0 38.7 %collective-permute-start.25 = (bf16[1040,256]{1,0:T(8,128)(2,1)S(1)}, bf16[1040,256]{1,0:T(8,128)(2,1)S(1)}, u32[]{:S(2)}, u32[]{:S(2)}) collective-permute-start(bf16[1040,256]{1,0:T(8,128)(2,1)S(1)} %shard_map.70), channel_id=1, source_target_pairs={{0,12},{4,0},{8,4},{12,8},{1,13},{5,1},{9,5},{13,9},{2,14},{6,2},{... | collective-permute-start | bytes 1597448 | tf_op jit(solution)/shard_map/ppermute | solution.py:101
  322.8 46.3 %collective-permute-start.24 = (bf16[1040,256]{1,0:T(8,128)(2,1)S(1)}, bf16[1040,256]{1,0:T(8,128)(2,1)S(1)}, u32[]{:S(2)}, u32[]{:S(2)}) collective-permute-start(bf16[1040,256]{1,0:T(8,128)(2,1)S(1)} %shard_map.69), channel_id=1, source_target_pairs={{0,4},{4,8},{8,12},{12,0},{1,5},{5,9},{9,13},{13,1},{2,6},{6,10},{... | collective-permute-start | bytes 1597448 | tf_op jit(solution)/shard_map/ppermute | solution.py:101
  331.6 71.5 %collective-permute-start.23 = (bf16[1040,256]{1,0:T(8,128)(2,1)S(1)}, bf16[1040,256]{1,0:T(8,128)(2,1)S(1)}, u32[]{:S(2)}, u32[]{:S(2)}) collective-permute-start(bf16[1040,256]{1,0:T(8,128)(2,1)S(1)} %shard_map.68), channel_id=1, source_target_pairs={{0,8},{4,12},{8,0},{12,4},{1,9},{5,13},{9,1},{13,5},{2,10},{6,14},... | collective-permute-start | bytes 1597448 | tf_op jit(solution)/shard_map/ppermute | solution.py:101
  358.6 45.7 %collective-permute-start.26 = (bf16[1024,256]{1,0:T(8,128)(2,1)S(1)}, bf16[1024,256]{1,0:T(8,128)(2,1)S(1)}, u32[]{:S(2)}, u32[]{:S(2)}) collective-permute-start(bf16[1024,256]{1,0:T(8,128)(2,1)S(1)} %fusion.205), channel_id=1, source_target_pairs={{0,16},{16,0},{1,17},{17,1},{2,18},{18,2},{3,19},{19,3},{4,20},{20... | collective-permute-start | bytes 1572872 | tf_op jit(solution)/shard_map/ppermute | solution.py:101
  (24 other events, 571.1 us)
Sparse Core Ops, SparseCore 0:
  36.1 48.0 all-gather.6
  87.7 47.0 all-gather.4
